TPU v7x, 128 devices: a whole 4x4x4 slice. The times are simulated.
128 devices in a mesh: segment: 2 (over core), cp: 16 (over x, z), tp: 4 (over y).
Axes of the slice: x: 4, y: 4, z: 4, core: 2. Of those that a mesh axis runs over, the one named last changes fastest.
Arguments:
- image_rows: bfloat16 [32, 801, 8192], P('cp', None, ('segment', 'tp')), may hold values from -6 to 6
- kv_weight: bfloat16 [8192, 2048], P(('segment', 'tp')), may hold values from -0.0625 to 0.0625
- k_gain: float32 [128], replicated, may hold values from 1 to 2.2
- tokens: bfloat16 [2048, 8192], P('cp', ('segment', 'tp')), may hold values from -6 to 6
- ln_gain: float32 [8192], replicated, may hold values from 0.1 to 1.9
- q_weight: bfloat16 [8192, 8192], P(None, ('segment', 'tp')), may hold values from -0.0625 to 0.0625
- q_gain: float32 [128], replicated, may hold values from 1 to 2.2
- image_doc: int32 [32], replicated, may hold values from 0 to 31, as said below
- doc_first: int32 [32], replicated, may hold values from 0 to 15, as said below
- doc_count: int32 [32], replicated, may hold values from 1 to 8, as said below
- token_mask: int32 [2048, 32], P('cp'), may hold values 0 or 1
Outputs:
- attended: bfloat16 [2048, 8192], P('cp', ('segment', 'tp'))
Inputs may be any that keep to these rules, and one draw needn't show every extreme that they name: `image_doc`: A permutation: each document holds exactly one image. `doc_first`: the documents of the 2 images of one context shard h (images h * 2 to h * 2 + 1) cover pairwise disjoint sets of context shards, so no context shard is covered by two images of the same shard. Some document starts on the last context shard. doc_first + doc_count never exceeds the number of context shards; some document covers exactly 16 // 2 shards and some exactly one.
All inputs are finite; a program needn't handle non-finite values. No bound on the sum of `token_mask` on one device may be relied on, other than what follows from the above.
Results may differ from a plain program's by a relative error of at most 0.034.
Values may be sent and summed in bfloat16 or wider, within the bound.
A program may use at most 128 MiB of HBM per device.

v0:
```python
import math

import jax
import jax.numpy as jnp
from jax import lax
from jax.sharding import PartitionSpec as P

EPSILON = 1e-06


def normalize(values_in):
    return values_in * lax.rsqrt(jnp.mean(values_in * values_in, axis=-1, keepdims=True) + EPSILON)


def per_device(
    image_rows,
    kv_weight,
    k_gain,
    tokens,
    ln_gain,
    q_weight,
    q_gain,
    image_doc,
    doc_first,
    doc_count,
    token_mask,
):
    head_dim = k_gain.shape[0]
    kv_cols = kv_weight.shape[1] // lax.axis_size(("segment", "tp"))
    kv_heads = kv_cols // (2 * head_dim)
    q_heads = q_weight.shape[1] // head_dim
    group_size = q_heads // kv_heads
    img_local = image_rows.shape[0]
    img_tok = image_rows.shape[1]
    tok_rows = tokens.shape[0]
    w_slice = kv_weight
    projected_cols = lax.psum_scatter(
        jnp.einsum("itv,vc->cit", image_rows, w_slice, preferred_element_type=jnp.float32).astype(
            jnp.bfloat16
        ),
        ("segment", "tp"),
        scatter_dimension=0,
        tiled=True,
    ).astype(jnp.float32)
    projected = jnp.transpose(projected_cols, (1, 2, 0))
    split_kv = projected.reshape(img_local, img_tok, kv_heads, 2, head_dim)
    key_part = (normalize(split_kv[:, :, :, 0]) * k_gain).astype(jnp.bfloat16)
    value_part = split_kv[:, :, :, 1].astype(jnp.bfloat16)
    slabs = jnp.stack([key_part, value_part], axis=3).reshape(img_local, img_tok, kv_cols)
    w_slice = q_weight
    query_raw = jnp.dot(
        (lax.all_gather(tokens, ("segment", "tp"), axis=1, tiled=True) * ln_gain).astype(
            jnp.bfloat16
        ),
        w_slice,
        preferred_element_type=jnp.float32,
    )
    query_raw = query_raw.reshape(tok_rows, kv_heads, group_size, head_dim)
    queries = (normalize(query_raw) * q_gain / math.sqrt(head_dim)).astype(jnp.bfloat16)
    n_docs = doc_first.shape[0]
    matches = image_doc[:, None] == jnp.arange(n_docs, dtype=jnp.int32)[None, :]
    doc_start = jnp.sum(jnp.where(matches, doc_first[None, :], 0), axis=1)
    doc_span = jnp.sum(jnp.where(matches, doc_count[None, :], 0), axis=1)
    my_shard = lax.axis_index("cp")
    covers = (doc_start <= my_shard) & (my_shard < doc_start + doc_span)
    tok_weight = token_mask.astype(jnp.float32) * covers.astype(jnp.float32)[None, :]

    def attend(carry_state, kv_slab, weight_now, used_now):

        def compute(current):
            numer, denom = current
            split_slab = kv_slab.reshape(img_tok, kv_heads, 2, head_dim)
            scores = jnp.einsum(
                "thgd,khd->thgk", queries, split_slab[:, :, 0], preferred_element_type=jnp.float32
            )
            weights_p = jnp.exp(scores) * weight_now[:, None, None, None]
            numer = numer + jnp.einsum(
                "thgk,khd->thgd",
                weights_p.astype(jnp.bfloat16),
                split_slab[:, :, 1],
                preferred_element_type=jnp.float32,
            )
            denom = denom + jnp.sum(weights_p, axis=-1)
            return (numer, denom)

        return lax.cond(used_now, compute, lambda current: current, carry_state)

    start_state = (
        jnp.zeros((tok_rows, kv_heads, group_size, head_dim), jnp.float32),
        jnp.zeros((tok_rows, kv_heads, group_size), jnp.float32),
    )
    block_part = lax.all_gather(slabs, "cp", axis=0, tiled=True)

    def advance(current, position):
        kv_slab = lax.dynamic_index_in_dim(block_part, position, 0, keepdims=False)
        weight_now = lax.dynamic_index_in_dim(tok_weight, position, 1, keepdims=False)
        used_now = lax.dynamic_index_in_dim(covers, position, 0, keepdims=False)
        return (attend(current, kv_slab, weight_now, used_now), None)

    result_state, _ = lax.scan(
        advance, start_state, jnp.arange(block_part.shape[0], dtype=jnp.int32)
    )
    numer, denom = result_state
    divisor = jnp.where(denom > 0, denom, 1.0)
    result = jnp.where(denom[..., None] > 0, numer / divisor[..., None], 0.0)
    return result.reshape(tok_rows, q_heads * head_dim).astype(jnp.bfloat16)


def solution(mesh):
    in_specs = (
        P("cp", None, ("segment", "tp")),
        P(("segment", "tp"), None),
        P(),
        P("cp", ("segment", "tp")),
        P(),
        P(None, ("segment", "tp")),
        P(),
        P(),
        P(),
        P(),
        P("cp", None),
    )
    out_specs = P("cp", ("segment", "tp"))
    return jax.shard_map(
        per_device, mesh=mesh, in_specs=in_specs, out_specs=out_specs, check_vma=False
    )
```

profile of v0, /device:TPU:3, one launch (start us, length us, event | category | flops | bytes accessed | tf_op | source)
XLA Modules:
  0.0 515.8 jit_solution(10648691951745002892)
XLA Ops:
  6.5 1.9 copy-done
  8.5 11.2 %convolution_convert_fusion = bf16[2048,2,801]{0,2,1:T(8,128)(2,1)} fusion(bf16[1024,2048]{1,0:T(8,128)(2,1)} %param.16, bf16[2,801,1024]{2,0,1:T(2,128)(2,1)S(1)} %copy-done), kind=kOutput, calls=%fused_computation.16 | convolution fusion | flops 6722555904 | bytes 14036992 | tf_op jit(solution)/shard_map/itv,vc->cit/dot_general | solution.py:38
  20.5 76.8 %reduce-scatter.2.cloned.1.call-done = bf16[256,2,801]{0,2,1:T(8,128)(2,1)} async-done(((bf16[2048,2,801]{0,2,1:T(8,128)(2,1)}), bf16[256,2,801]{0,2,1:T(8,128)(2,1)}) %reduce-scatter.2.cloned.1.call-update) | async-done | bytes 820240 | tf_op jit(solution)/shard_map/reduce_scatter | solution.py:37
  97.3 3.0 reshape.172
  100.3 2.1 slice.26
  102.4 4.6 multiply_reduce_fusion
  107.0 4.2 multiply_convert_fusion.4
  111.2 2.8 pad_maximum_fusion
  114.0 3.5 reshape.173
  118.4 6.0 %all-gather.5.cloned.1.call-done = bf16[128,8192]{1,0:T(8,128)(2,1)} async-done(((bf16[128,1024]{1,0:T(8,128)(2,1)}), bf16[128,8192]{1,0:T(8,128)(2,1)}) %all-gather.5.cloned.1.call-update) | async-done | bytes 2097168 | tf_op jit(solution)/shard_map/all_gather | solution.py:52
  124.4 8.7 %fusion.17 = f32[16,8,8,128]{3,1,2,0:T(8,128)S(1)} fusion(bf16[8192,1024]{1,0:T(8,128)(2,1)} %param.20, bf16[128,8192]{1,0:T(8,128)(2,1)} %all-gather.5.cloned.1.call-done, f32[8192]{0:T(1024)S(1)} %copy-done.4), kind=kOutput, calls=%fused_computation.22 | convolution fusion | flops 2150629376 | bytes 19431424 | tf_op jit(solution)/shard_map/dot_general | solution.py:51
  135.6 84.4 %all-gather.3.cloned.1.call-done = bf16[32,801,256]{2,1,0:T(8,128)(2,1)} async-done(((bf16[2,801,256]{2,1,0:T(8,128)(2,1)}), bf16[32,801,256]{2,1,0:T(8,128)(2,1)}) %all-gather.3.cloned.1.call-update) | async-done | bytes 13123600 | tf_op jit(solution)/shard_map/all_gather | solution.py:92
  221.4 285.8 %while.12 = (s32[]{:T(128)}, f32[128,1,8,128]{0,3,2,1:T(8,128)}, f32[128,1,8]{0,2,1:T(8,128)S(1)}, s32[32]{0:T(128)}, pred[32]{0:T(512)(128)(4,1)S(1)}, /*index=...) while((s32[]{:T(128)}, f32[128,1,8,128]{0,3,2,1:T(8,128)}, ...), condition=%wide.region_9.10_spmd, body=%wide.region_5.9_spmd.sunk | while | flops 423366656 | bytes 14956358 | solution.py:100
  226.2 8.9 %conditional.2 = ((f32[128,1,8,128]{0,3,2,1:T(8,128)}, f32[128,1,8]{0,2,1:T(8,128)S(1)})) conditional(s32[]{:T(128)} %bitcast.79, (f32[128,1,8,128]{0,3,2,1:T(8,128)}, f32[128,1,8]{0,2,1:T(8,128)S(1)}) %tuple.35, (bf16[32,801,256]{2,1,0:T(8,128)(2,1)}, s32[]{:T(128)}, bf16[128,1,8,128]{3,0,2,1:T(8,128)(2,1)S(1)}, f32[128,32]{0,1:T(8,128)}, ...), branch_computations={%region_6.6_spmd, %region_7.8_spmd} | conditional | flops 423366656 | bytes 14956120 | solution.py:86
  228.7 2.2 reshape.164
  230.9 1.9 fusion.23
  249.4 8.9 %conditional.2 = ((f32[128,1,8,128]{0,3,2,1:T(8,128)}, f32[128,1,8]{0,2,1:T(8,128)S(1)})) conditional(s32[]{:T(128)} %bitcast.79, (f32[128,1,8,128]{0,3,2,1:T(8,128)}, f32[128,1,8]{0,2,1:T(8,128)S(1)}) %tuple.35, (bf16[32,801,256]{2,1,0:T(8,128)(2,1)}, s32[]{:T(128)}, bf16[128,1,8,128]{3,0,2,1:T(8,128)(2,1)S(1)}, f32[128,32]{0,1:T(8,128)}, ...), branch_computations={%region_6.6_spmd, %region_7.8_spmd} | conditional | flops 423366656 | bytes 14956120 | solution.py:86
  251.9 2.2 reshape.164
  254.1 1.9 fusion.23
  267.8 8.9 %conditional.2 = ((f32[128,1,8,128]{0,3,2,1:T(8,128)}, f32[128,1,8]{0,2,1:T(8,128)S(1)})) conditional(s32[]{:T(128)} %bitcast.79, (f32[128,1,8,128]{0,3,2,1:T(8,128)}, f32[128,1,8]{0,2,1:T(8,128)S(1)}) %tuple.35, (bf16[32,801,256]{2,1,0:T(8,128)(2,1)}, s32[]{:T(128)}, bf16[128,1,8,128]{3,0,2,1:T(8,128)(2,1)S(1)}, f32[128,32]{0,1:T(8,128)}, ...), branch_computations={%region_6.6_spmd, %region_7.8_spmd} | conditional | flops 423366656 | bytes 14956120 | solution.py:86
  270.3 2.2 reshape.164
  272.5 1.9 fusion.23
  281.4 8.9 %conditional.2 = ((f32[128,1,8,128]{0,3,2,1:T(8,128)}, f32[128,1,8]{0,2,1:T(8,128)S(1)})) conditional(s32[]{:T(128)} %bitcast.79, (f32[128,1,8,128]{0,3,2,1:T(8,128)}, f32[128,1,8]{0,2,1:T(8,128)S(1)}) %tuple.35, (bf16[32,801,256]{2,1,0:T(8,128)(2,1)}, s32[]{:T(128)}, bf16[128,1,8,128]{3,0,2,1:T(8,128)(2,1)S(1)}, f32[128,32]{0,1:T(8,128)}, ...), branch_computations={%region_6.6_spmd, %region_7.8_spmd} | conditional | flops 423366656 | bytes 14956120 | solution.py:86
  283.9 2.2 reshape.164
  286.1 1.9 fusion.23
  299.9 8.9 %conditional.2 = ((f32[128,1,8,128]{0,3,2,1:T(8,128)}, f32[128,1,8]{0,2,1:T(8,128)S(1)})) conditional(s32[]{:T(128)} %bitcast.79, (f32[128,1,8,128]{0,3,2,1:T(8,128)}, f32[128,1,8]{0,2,1:T(8,128)S(1)}) %tuple.35, (bf16[32,801,256]{2,1,0:T(8,128)(2,1)}, s32[]{:T(128)}, bf16[128,1,8,128]{3,0,2,1:T(8,128)(2,1)S(1)}, f32[128,32]{0,1:T(8,128)}, ...), branch_computations={%region_6.6_spmd, %region_7.8_spmd} | conditional | flops 423366656 | bytes 14956120 | solution.py:86
  302.4 2.2 reshape.164
  318.3 8.9 %conditional.2 = ((f32[128,1,8,128]{0,3,2,1:T(8,128)}, f32[128,1,8]{0,2,1:T(8,128)S(1)})) conditional(s32[]{:T(128)} %bitcast.79, (f32[128,1,8,128]{0,3,2,1:T(8,128)}, f32[128,1,8]{0,2,1:T(8,128)S(1)}) %tuple.35, (bf16[32,801,256]{2,1,0:T(8,128)(2,1)}, s32[]{:T(128)}, bf16[128,1,8,128]{3,0,2,1:T(8,128)(2,1)S(1)}, f32[128,32]{0,1:T(8,128)}, ...), branch_computations={%region_6.6_spmd, %region_7.8_spmd} | conditional | flops 423366656 | bytes 14956120 | solution.py:86
  320.8 2.2 reshape.164
  341.5 8.9 %conditional.2 = ((f32[128,1,8,128]{0,3,2,1:T(8,128)}, f32[128,1,8]{0,2,1:T(8,128)S(1)})) conditional(s32[]{:T(128)} %bitcast.79, (f32[128,1,8,128]{0,3,2,1:T(8,128)}, f32[128,1,8]{0,2,1:T(8,128)S(1)}) %tuple.35, (bf16[32,801,256]{2,1,0:T(8,128)(2,1)}, s32[]{:T(128)}, bf16[128,1,8,128]{3,0,2,1:T(8,128)(2,1)S(1)}, f32[128,32]{0,1:T(8,128)}, ...), branch_computations={%region_6.6_spmd, %region_7.8_spmd} | conditional | flops 423366656 | bytes 14956120 | solution.py:86
  344.0 2.2 reshape.164
  355.1 8.9 %conditional.2 = ((f32[128,1,8,128]{0,3,2,1:T(8,128)}, f32[128,1,8]{0,2,1:T(8,128)S(1)})) conditional(s32[]{:T(128)} %bitcast.79, (f32[128,1,8,128]{0,3,2,1:T(8,128)}, f32[128,1,8]{0,2,1:T(8,128)S(1)}) %tuple.35, (bf16[32,801,256]{2,1,0:T(8,128)(2,1)}, s32[]{:T(128)}, bf16[128,1,8,128]{3,0,2,1:T(8,128)(2,1)S(1)}, f32[128,32]{0,1:T(8,128)}, ...), branch_computations={%region_6.6_spmd, %region_7.8_spmd} | conditional | flops 423366656 | bytes 14956120 | solution.py:86
  357.6 2.2 reshape.164
  378.3 8.9 %conditional.2 = ((f32[128,1,8,128]{0,3,2,1:T(8,128)}, f32[128,1,8]{0,2,1:T(8,128)S(1)})) conditional(s32[]{:T(128)} %bitcast.79, (f32[128,1,8,128]{0,3,2,1:T(8,128)}, f32[128,1,8]{0,2,1:T(8,128)S(1)}) %tuple.35, (bf16[32,801,256]{2,1,0:T(8,128)(2,1)}, s32[]{:T(128)}, bf16[128,1,8,128]{3,0,2,1:T(8,128)(2,1)S(1)}, f32[128,32]{0,1:T(8,128)}, ...), branch_computations={%region_6.6_spmd, %region_7.8_spmd} | conditional | flops 423366656 | bytes 14956120 | solution.py:86
  380.8 2.2 reshape.164
  392.0 8.9 %conditional.2 = ((f32[128,1,8,128]{0,3,2,1:T(8,128)}, f32[128,1,8]{0,2,1:T(8,128)S(1)})) conditional(s32[]{:T(128)} %bitcast.79, (f32[128,1,8,128]{0,3,2,1:T(8,128)}, f32[128,1,8]{0,2,1:T(8,128)S(1)}) %tuple.35, (bf16[32,801,256]{2,1,0:T(8,128)(2,1)}, s32[]{:T(128)}, bf16[128,1,8,128]{3,0,2,1:T(8,128)(2,1)S(1)}, f32[128,32]{0,1:T(8,128)}, ...), branch_computations={%region_6.6_spmd, %region_7.8_spmd} | conditional | flops 423366656 | bytes 14956120 | solution.py:86
  394.5 2.2 reshape.164
  415.2 8.9 %conditional.2 = ((f32[128,1,8,128]{0,3,2,1:T(8,128)}, f32[128,1,8]{0,2,1:T(8,128)S(1)})) conditional(s32[]{:T(128)} %bitcast.79, (f32[128,1,8,128]{0,3,2,1:T(8,128)}, f32[128,1,8]{0,2,1:T(8,128)S(1)}) %tuple.35, (bf16[32,801,256]{2,1,0:T(8,128)(2,1)}, s32[]{:T(128)}, bf16[128,1,8,128]{3,0,2,1:T(8,128)(2,1)S(1)}, f32[128,32]{0,1:T(8,128)}, ...), branch_computations={%region_6.6_spmd, %region_7.8_spmd} | conditional | flops 423366656 | bytes 14956120 | solution.py:86
  417.7 2.2 reshape.164
  443.1 8.9 %conditional.2 = ((f32[128,1,8,128]{0,3,2,1:T(8,128)}, f32[128,1,8]{0,2,1:T(8,128)S(1)})) conditional(s32[]{:T(128)} %bitcast.79, (f32[128,1,8,128]{0,3,2,1:T(8,128)}, f32[128,1,8]{0,2,1:T(8,128)S(1)}) %tuple.35, (bf16[32,801,256]{2,1,0:T(8,128)(2,1)}, s32[]{:T(128)}, bf16[128,1,8,128]{3,0,2,1:T(8,128)(2,1)S(1)}, f32[128,32]{0,1:T(8,128)}, ...), branch_computations={%region_6.6_spmd, %region_7.8_spmd} | conditional | flops 423366656 | bytes 14956120 | solution.py:86
  445.6 2.2 reshape.164
  447.8 1.9 fusion.23
  461.6 8.9 %conditional.2 = ((f32[128,1,8,128]{0,3,2,1:T(8,128)}, f32[128,1,8]{0,2,1:T(8,128)S(1)})) conditional(s32[]{:T(128)} %bitcast.79, (f32[128,1,8,128]{0,3,2,1:T(8,128)}, f32[128,1,8]{0,2,1:T(8,128)S(1)}) %tuple.35, (bf16[32,801,256]{2,1,0:T(8,128)(2,1)}, s32[]{:T(128)}, bf16[128,1,8,128]{3,0,2,1:T(8,128)(2,1)S(1)}, f32[128,32]{0,1:T(8,128)}, ...), branch_computations={%region_6.6_spmd, %region_7.8_spmd} | conditional | flops 423366656 | bytes 14956120 | solution.py:86
  464.1 2.2 reshape.164
  480.0 8.9 %conditional.2 = ((f32[128,1,8,128]{0,3,2,1:T(8,128)}, f32[128,1,8]{0,2,1:T(8,128)S(1)})) conditional(s32[]{:T(128)} %bitcast.79, (f32[128,1,8,128]{0,3,2,1:T(8,128)}, f32[128,1,8]{0,2,1:T(8,128)S(1)}) %tuple.35, (bf16[32,801,256]{2,1,0:T(8,128)(2,1)}, s32[]{:T(128)}, bf16[128,1,8,128]{3,0,2,1:T(8,128)(2,1)S(1)}, f32[128,32]{0,1:T(8,128)}, ...), branch_computations={%region_6.6_spmd, %region_7.8_spmd} | conditional | flops 423366656 | bytes 14956120 | solution.py:86
  482.5 2.2 reshape.164
  498.4 8.9 %conditional.2 = ((f32[128,1,8,128]{0,3,2,1:T(8,128)}, f32[128,1,8]{0,2,1:T(8,128)S(1)})) conditional(s32[]{:T(128)} %bitcast.79, (f32[128,1,8,128]{0,3,2,1:T(8,128)}, f32[128,1,8]{0,2,1:T(8,128)S(1)}) %tuple.35, (bf16[32,801,256]{2,1,0:T(8,128)(2,1)}, s32[]{:T(128)}, bf16[128,1,8,128]{3,0,2,1:T(8,128)(2,1)S(1)}, f32[128,32]{0,1:T(8,128)}, ...), branch_computations={%region_6.6_spmd, %region_7.8_spmd} | conditional | flops 423366656 | bytes 14956120 | solution.py:86
  500.9 2.2 reshape.164
  (265 shorter events, 161.4 us)
Async XLA Ops:
  6.5 1.9 copy-start
  6.5 90.7 %reduce-scatter.2.cloned.1.call-start = ((), (), s32[]{:S(2)}) async-start(), calls=%async_computation.1 | async-start | bytes 7446528 | tf_op jit(solution)/shard_map/reduce_scatter | solution.py:37
  19.7 87.3 %copy-start.6 = (f32[128]{0:T(128)S(1)}, f32[128]{0:T(128)}, u32[]{:S(2)}) copy-start(f32[128]{0:T(128)} %param.17) | copy-start | bytes 1540
  19.7 104.7 %all-gather.5.cloned.1.call-start = ((), (), s32[]{:S(2)}) async-start(), calls=%async_computation.3 | async-start | bytes 2359296 | tf_op jit(solution)/shard_map/all_gather | solution.py:52
  20.4 199.6 %all-gather.3.cloned.1.call-start = ((), (), s32[]{:S(2)}) async-start(), calls=%async_computation.2 | async-start | bytes 14065664 | tf_op jit(solution)/shard_map/all_gather | solution.py:92
  106.9 10.6 %copy-start.7 = (s32[32]{0:T(128)S(1)}, s32[32]{0:T(128)}, u32[]{:S(2)}) copy-start(s32[32]{0:T(128)} %param.24) | copy-start | bytes 388
  106.9 10.6 %copy-start.8 = (s32[32]{0:T(128)S(1)}, s32[32]{0:T(128)}, u32[]{:S(2)}) copy-start(s32[32]{0:T(128)} %param.22) | copy-start | bytes 388
  106.9 10.6 %copy-start.9 = (s32[32]{0:T(128)S(1)}, s32[32]{0:T(128)}, u32[]{:S(2)}) copy-start(s32[32]{0:T(128)} %param.23) | copy-start | bytes 388
  106.9 10.8 %copy-start.5 = (s32[128,32]{0,1:T(8,128)S(1)}, s32[128,32]{0,1:T(8,128)}, u32[]{:S(2)}) copy-start(s32[128,32]{0,1:T(8,128)} %param.25) | copy-start | bytes 49156
  107.0 17.4 %copy-start.4 = (f32[8192]{0:T(1024)S(1)}, f32[8192]{0:T(1024)}, u32[]{:S(2)}) copy-start(f32[8192]{0:T(1024)} %param.19) | copy-start | bytes 98308
  118.4 15.9 %copy-start.10 = (f32[128]{0:T(128)S(1)}, f32[128]{0:T(128)}, u32[]{:S(2)}) copy-start(f32[128]{0:T(128)} %param.21) | copy-start | bytes 1540
  133.2 0.8 copy-start.3
  230.9 2.6 copy-start.1
  234.3 0.8 copy-start.2
  254.1 2.6 copy-start.1
  257.5 0.8 copy-start.2
  272.5 2.6 copy-start.1
  275.9 0.8 copy-start.2
  286.1 2.6 copy-start.1
  289.5 0.8 copy-start.2
  304.6 2.6 copy-start.1
  307.9 0.8 copy-start.2
  323.0 2.6 copy-start.1
  326.4 0.8 copy-start.2
  346.2 2.6 copy-start.1
  349.6 0.8 copy-start.2
  359.8 2.6 copy-start.1
  363.2 0.8 copy-start.2
  383.0 2.6 copy-start.1
  386.4 0.8 copy-start.2
  396.7 2.6 copy-start.1
  400.0 0.8 copy-start.2
  419.9 2.6 copy-start.1
  423.2 0.8 copy-start.2
  447.8 2.6 copy-start.1
  451.2 0.8 copy-start.2
  466.3 2.6 copy-start.1
  469.6 0.8 copy-start.2
  484.7 2.6 copy-start.1
  488.1 0.8 copy-start.2
  503.1 2.6 copy-start.1
  506.5 0.8 copy-start.2
Sparse Core Ops, SparseCore 0:
  19.8 77.4 reduce-scatter.1
  99.1 25.2 all-gather.4
  126.8 93.1 all-gather.2
where the time goes:
time: 520 us; the launch traced here: 516 us
  local copies, waits for them, and re-layouts  188 us (36%)
  waiting for transfers between devices  168 us (32%)
  loops' own time  89.8 us (17%)
  matrix products  41.7 us (8%)
  other arithmetic  15.1 us (3%)
  between operations  13.3 us (3%)
    another operation x1, loops' own time, per_device(): lax.scan(advance, start_state, jnp.arange(block_part.shape[0], dtype=jnp....  88.7 us
    all_gather x1, waiting for transfers between devices, per_device(): block_part = lax.all_gather(slabs, 'cp', axis=0, tiled=True)  84.4 us
    reduce_scatter x1, waiting for transfers between devices, per_device(): lax.psum_scatter(jnp.einsum('itv,vc->cit', image_rows, w_slice, preferred...  76.8 us
    dynamic_slice x32, local copies, waits for them, and re-layouts, per_device(): lax.scan(advance, start_state, jnp.arange(block_part.shape[0], dtype=jnp....  42.1 us
    reshape x15, local copies, waits for them, and re-layouts, compute(): split_slab = kv_slab.reshape(img_tok, kv_heads, 2, head_dim)  32.9 us
    slice x15, local copies, waits for them, and re-layouts, compute(): split_slab[:, :, 1]  28.3 us
    dynamic_slice x15, local copies, waits for them, and re-layouts, advance(): kv_slab = lax.dynamic_index_in_dim(block_part, position, 0, keepdims=False)  26.9 us
    dynamic_slice x32, local copies, waits for them, and re-layouts, advance(): used_now = lax.dynamic_index_in_dim(covers, position, 0, keepdims=False)  21.3 us
  transfers between devices with their start and end apart: 3, of which 3 were waited for; matrix products, arithmetic and copies ran while one was open for 6% of the time, Pallas kernels for 0%

commit v1 on v0

v1 whole, which is shorter than its diff:
```python
import functools
import math

import jax
import jax.numpy as jnp
from jax import lax
from jax.experimental import pallas as pl
from jax.experimental.pallas import tpu as pltpu
from jax.sharding import PartitionSpec as P

EPSILON = 1e-06
MESH = pl.DeviceIdType.MESH
BF16 = jnp.bfloat16
F32 = jnp.float32

RING = 4
SHARDS = 16
TOK = 128
HD = 128
IMG_TOK = 801
KV_ROWS = 816
KEYS = 896
HALF = 528
CUT = 256

KV_ORDER = ((2, 0), (2, 1), (1, 1), (3, 0), (1, 0), (3, 1), (0, 0), (0, 1))
UNITS = (
    (2, 2), (2, 1), (1, 2), (2, 3), (3, 2), (2, 0), (0, 2), (1, 1),
    (3, 3), (1, 3), (3, 1), (1, 0), (0, 1), (3, 0), (0, 3), (0, 0),
)
FAR_LAG = 3
NEAR_LAG = 5


def pick(index, values):
    return sum((index == at).astype(jnp.int32) * value for at, value in enumerate(values) if value)


def lay_out(unit_of):
    steps = []
    order = 0

    def add(slot, kind, half, dg):
        nonlocal order
        steps.append((slot, order, kind, half, dg))
        order += 1

    for half in (0, 1):
        unit = lambda df, dg: unit_of[(dg, df) if half == 0 else (df, dg)]
        total_at = {}
        for dg in (2, 1, 3, 0):
            far = unit(2, dg)
            add(far, "far", half, dg)
            up = max(unit(1, dg), far + FAR_LAG)
            down = max(unit(3, dg), far + FAR_LAG)
            add(up, "up", half, dg)
            add(down, "down", half, dg)
            total_at[dg] = max(unit(0, dg), max(up, down) + NEAR_LAG)
            add(total_at[dg], "total", half, dg)
        add(total_at[2], "gfar", half, 2)
        add(max(total_at[1], total_at[2] + FAR_LAG), "gup", half, 1)
        add(max(total_at[3], total_at[2] + FAR_LAG), "gdown", half, 3)
    return sorted(steps)


def kernel(
    x_hbm, w_hbm, kg_ref, tok_ref, ln_ref, wq_hbm, qg_ref, doc_ref, first_ref, count_ref, mask_ref,
    out_ref,
    xs, ws, wq, tok, cs, cr, mine, yr, acc, qall, kb, vb, pb, rf, rn, rgf, rgn, total,
    load_sem, send_sem, recv_sem,
):
    s = lax.axis_index("segment")
    cp = lax.axis_index("cp")
    t = lax.axis_index("tp")
    x, z = cp // RING, cp % RING

    def plus(v, n):
        return lax.rem(v + n, RING)

    peers = {
        "c": (1 - s, cp, t),
        "y+": (s, cp, plus(t, 1)),
        "y-": (s, cp, plus(t, 3)),
        "x+": (s, plus(x, 1) * RING + z, t),
        "x-": (s, plus(x, 3) * RING + z, t),
        "z+": (s, x * RING + plus(z, 1), t),
        "z-": (s, x * RING + plus(z, 3), t),
    }

    numbers = {}

    def number(key):
        return numbers.setdefault(key, len(numbers))

    started = []

    def copy_of(key, src, dst, peer):
        n = number(key) if isinstance(key, tuple) else key
        return pltpu.make_async_remote_copy(
            src_ref=src, dst_ref=dst, send_sem=send_sem.at[n], recv_sem=recv_sem.at[n],
            device_id=peers[peer], device_id_type=MESH,
        )

    def send(key, src, dst, peer):
        copy_of(key, src(), dst(), peer).start()
        started.append((key, src, dst, peer))

    def arrived(key, dst):
        copy_of(key, dst, dst, "c").wait_recv()

    def load(n, src, dst):
        return pltpu.make_async_copy(src, dst, load_sem.at[n])

    def head_cols(head):
        return pl.ds(pl.multiple_of(head * 2 * HD, 2 * HD), 2 * HD)

    x_loads = [load(i, x_hbm.at[i], xs.at[i]) for i in range(2)]
    w_loads = {}
    for at, dt in enumerate((2, 1, 3, 0)):
        for other in (1, 0):
            head = (1 - s if other else s) * RING + plus(t, dt)
            w_loads[dt, other] = load(
                2 + at * 2 + (1 - other), w_hbm.at[:, head_cols(head)], ws.at[at * 2 + (1 - other)]
            )
    tok_order = ((0, 0), (1, 0), (0, 3), (0, 1), (1, 3), (1, 1), (0, 2), (1, 2))
    blocks = [(1 - s if o else s) * RING + plus(t, dt) for o, dt in tok_order]
    width = wq.shape[0] // 8
    wq_loads = [
        load(10 + n, wq_hbm.at[pl.ds(pl.multiple_of(b * width, width), width)], wq.at[pl.ds(n * width, width)])
        for n, b in enumerate(blocks)
    ]
    x_loads[0].start()
    w_loads[2, 1].start()
    w_loads[2, 0].start()
    x_loads[1].start()
    for dt in (1, 3, 0):
        w_loads[dt, 1].start()
        w_loads[dt, 0].start()
    for copy in wq_loads:
        copy.start()

    barrier = pltpu.get_barrier_semaphore()
    for peer in peers.values():
        pl.semaphore_signal(barrier, inc=1, device_id=peer, device_id_type=MESH)

    gain = ln_ref[s * RING + t]
    for c in range(8):
        cols = slice(c * 128, (c + 1) * 128)
        tok[0, :, cols] = (tok_ref[:, cols].astype(F32) * gain[c : c + 1, :]).astype(BF16)
    pl.semaphore_wait(barrier, len(peers))

    send(("tok", "y+"), lambda: tok.at[0], lambda: tok.at[2], "y+")
    send(("tok", "y-"), lambda: tok.at[0], lambda: tok.at[3], "y-")
    send(("tok", "c0"), lambda: tok.at[0], lambda: tok.at[1], "c")

    cut = 400
    kv_c = [number(("kvc", k)) for k in range(8)]
    assert kv_c == list(range(kv_c[0], kv_c[0] + 8))

    def kv_slot(k, carry):
        dt_at = pick(k, [(2, 1, 3, 0).index(dt) for dt, _ in KV_ORDER])
        img = pick(k, [i for _, i in KV_ORDER])

        @pl.when(k == 0)
        def _():
            x_loads[0].wait()
            w_loads[2, 1].wait()
            w_loads[2, 0].wait()

        @pl.when(k == 1)
        def _():
            x_loads[1].wait()

        for first_use, dt in ((2, 1), (3, 3), (6, 0)):
            @pl.when(k == first_use)
            def _():
                w_loads[dt, 1].wait()
                w_loads[dt, 0].wait()

        for which, dst in ((0, cs), (1, mine)):
            dst[k, 800:, :] = jnp.zeros((KV_ROWS - 800, 2 * HD), BF16)
            weight = ws[dt_at * 2 + which]
            for lo, hi in ((0, cut), (cut, IMG_TOK)):
                dst[k, lo:hi, :] = jnp.dot(xs[img, lo:hi, :], weight, preferred_element_type=F32).astype(BF16)
            if which == 0:
                copy_of(kv_c[0] + k, cs.at[k], cr.at[k], "c").start()

        @pl.when(k > 0)
        def _():
            before = k - 1
            arrived(kv_c[0] + before, cr.at[before])
            mine[before] = (mine[before].astype(F32) + cr[before].astype(F32)).astype(BF16)

        return carry

    lax.fori_loop(0, 5, kv_slot, 0)

    half_tok = TOK // 2
    arrived(("tok", "y+"), tok.at[2])
    send(("tokf", "y+"), lambda: tok.at[2, 0:half_tok], lambda: tok.at[6, 0:half_tok], "y+")
    send(("tok", "c2"), lambda: tok.at[2], lambda: tok.at[4], "c")
    arrived(("tok", "y-"), tok.at[3])
    send(("tokf", "y-"), lambda: tok.at[3, half_tok:], lambda: tok.at[6, half_tok:], "y-")
    send(("tok", "c3"), lambda: tok.at[3], lambda: tok.at[5], "c")

    lax.fori_loop(5, 8, kv_slot, 0)

    send(("kv", "far", 0), lambda: mine.at[0], lambda: yr.at[0], "y+")
    send(("kv", "far", 1), lambda: mine.at[1], lambda: yr.at[1], "y-")
    arrived(kv_c[7], cr.at[7])
    mine[7] = (mine[7].astype(F32) + cr[7].astype(F32)).astype(BF16)

    arrived(("tok", "c0"), tok.at[1])
    arrived(("tok", "c2"), tok.at[4])
    arrived(("tok", "c3"), tok.at[5])
    acc[...] = jnp.zeros_like(acc)

    def project(n, carry):
        for m in range(8):
            @pl.when(n == m)
            def _():
                wq_loads[m].wait()

        rows = pl.ds(pl.multiple_of(n * width, width), width)
        acc[...] += jnp.dot(tok[n], wq[rows, :], preferred_element_type=F32)
        return carry

    lax.fori_loop(0, 6, project, 0)
    send(("kv", "near", 1, 1), lambda: mine.at[2], lambda: yr.at[3], "y+")
    send(("kv", "near", 3, 0), lambda: mine.at[3], lambda: yr.at[4], "y-")
    arrived(("tokf", "y+"), tok.at[6, 0:half_tok])
    arrived(("tokf", "y-"), tok.at[6, half_tok:])
    send(("tok", "c6"), lambda: tok.at[6], lambda: tok.at[7], "c")
    arrived(("tok", "c6"), tok.at[7])
    lax.fori_loop(6, 8, project, 0)

    eye = (
        lax.broadcasted_iota(jnp.int32, (HD, HD), 0) == lax.broadcasted_iota(jnp.int32, (HD, HD), 1)
    ).astype(F32)
    q_scale = qg_ref[...] * (math.log2(math.e) / math.sqrt(HD))
    for g in range(8):
        raw = acc[:, g * HD : (g + 1) * HD]
        inv = lax.rsqrt(jnp.mean(raw * raw, axis=-1, keepdims=True) + EPSILON)
        qall[cp, g // 4, (g % 4) * TOK : (g % 4 + 1) * TOK, :] = (raw * inv * q_scale).astype(BF16)
    eye_img = eye[:32, :32].astype(BF16)
    mask_rows = lax.dot_general(
        eye_img, mask_ref[...].astype(F32).astype(BF16), (((1,), (1,)), ((), ())), preferred_element_type=F32
    )
    for half in (0, 1):
        qall[cp, half, 512:, :] = mask_rows[half * 16 : (half + 1) * 16, :].astype(BF16)

    def shard(half, da, db):
        dx, dz = (da, db) if half == 0 else (db, da)
        return plus(x, dx) * RING + plus(z, dz)

    axes = (("x", "z"), ("z", "x"))
    lower, upper = pl.ds(0, CUT), pl.ds(CUT, HALF - CUT)

    def forward(tag, half, block, peer, rows=None):
        ref = lambda: qall.at[block, half] if rows is None else qall.at[block, half, rows]
        send(("q", half) + tag, ref, ref, peer)

    def q_arrived(tag, half, block, rows=None):
        ref = qall.at[block, half] if rows is None else qall.at[block, half, rows]
        arrived(("q", half) + tag, ref)

    for half in (0, 1):
        a, b = axes[half]
        forward(("a", 0), half, cp, a + "+")
        forward(("a", 1), half, cp, a + "-")
    for half in (0, 1):
        a, b = axes[half]
        forward(("b", 0, 0), half, cp, b + "+")
        forward(("b", 0, 1), half, cp, b + "-")

    arrived(("kv", "far", 0), yr.at[0])
    mine[4] = (mine[4].astype(F32) + yr[0].astype(F32)).astype(BF16)
    send(("kv", "near", 1, 0), lambda: mine.at[4], lambda: yr.at[2], "y+")
    arrived(("kv", "far", 1), yr.at[1])
    mine[5] = (mine[5].astype(F32) + yr[1].astype(F32)).astype(BF16)
    send(("kv", "near", 3, 1), lambda: mine.at[5], lambda: yr.at[5], "y-")

    for half in (0, 1):
        a, b = axes[half]
        q_arrived(("a", 0), half, shard(half, 3, 0))
        forward(("af", 0), half, shard(half, 3, 0), a + "+", lower)
        q_arrived(("a", 1), half, shard(half, 1, 0))
        forward(("af", 1), half, shard(half, 1, 0), a + "-", upper)
    for half in (0, 1):
        a, b = axes[half]
        for da in (3, 1):
            forward(("b", da, 0), half, shard(half, da, 0), b + "+")
            forward(("b", da, 1), half, shard(half, da, 0), b + "-")

    def pass_on(half, da):
        b = axes[half][1]
        q_arrived(("b", da, 0), half, shard(half, da, 3))
        forward(("bf", da, 0), half, shard(half, da, 3), b + "+", lower)
        q_arrived(("b", da, 1), half, shard(half, da, 1))
        forward(("bf", da, 1), half, shard(half, da, 1), b + "-", upper)

    for half in (0, 1):
        pass_on(half, 0)
    for half in (0, 1):
        a, b = axes[half]
        q_arrived(("af", 0), half, shard(half, 2, 0), lower)
        q_arrived(("af", 1), half, shard(half, 2, 0), upper)
        forward(("b", 2, 0), half, shard(half, 2, 0), b + "+")
        forward(("b", 2, 1), half, shard(half, 2, 0), b + "-")
    for da in (3, 1, 2):
        for half in (0, 1):
            pass_on(half, da)

    live = lax.broadcasted_iota(jnp.int32, (KV_ROWS, HD), 0) < IMG_TOK
    for img in (0, 1):
        kb[img, KV_ROWS:, :] = jnp.zeros((KEYS - KV_ROWS, HD), BF16)
        vb[img, KV_ROWS:, :] = jnp.zeros((KEYS - KV_ROWS, 2 * HD), BF16)
        vb[img, :KV_ROWS, HD:] = jnp.where(live, 1.0, 0.0).astype(BF16)
    for img in (1, 0):
        arrived(("kv", "near", 1, img), yr.at[2 + img])
        arrived(("kv", "near", 3, img), yr.at[4 + img])
        keys = (
            mine[6 + img, :, :HD].astype(F32) + yr[2 + img, :, :HD].astype(F32) + yr[4 + img, :, :HD].astype(F32)
        )
        inv = lax.rsqrt(jnp.mean(keys * keys, axis=-1, keepdims=True) + EPSILON)
        kb[img, :KV_ROWS, :] = jnp.where(live, keys * inv * kg_ref[...], 0.0).astype(BF16)
        values = (
            mine[6 + img, :, HD:].astype(F32) + yr[2 + img, :, HD:].astype(F32) + yr[4 + img, :, HD:].astype(F32)
        )
        vb[img, :KV_ROWS, :HD] = jnp.where(live, values, 0.0).astype(BF16)

    for da in (0, 3, 1, 2):
        for half in (0, 1):
            q_arrived(("bf", da, 0), half, shard(half, da, 2), lower)
            q_arrived(("bf", da, 1), half, shard(half, da, 2), upper)

    unit_of = {offset: u for u, offset in enumerate(UNITS)}
    rs_axes = (("z", "x"), ("x", "z"))

    def block(half, df, dg):
        return pb.at[half, unit_of[(dg, df) if half == 0 else (df, dg)]]

    def add_rows(ref, rows, other):
        ref[rows, :] = (ref[rows, :].astype(F32) + other[rows, :].astype(F32)).astype(BF16)

    def do(kind, half, dg):
        f, g = rs_axes[half]
        if kind == "far":
            ref, dst = lambda: block(half, 2, dg), lambda: rf.at[half, dg]
            send(("n", half, dg, "f0"), lambda: ref().at[lower], lambda: dst().at[lower], f + "+")
            send(("n", half, dg, "f1"), lambda: ref().at[upper], lambda: dst().at[upper], f + "-")
        elif kind == "up":
            arrived(("n", half, dg, "f0"), rf.at[half, dg, lower])
            add_rows(block(half, 1, dg), lower, rf.at[half, dg])
            send(("n", half, dg, "u"), lambda: block(half, 1, dg), lambda: rn.at[half, dg, 0], f + "+")
        elif kind == "down":
            arrived(("n", half, dg, "f1"), rf.at[half, dg, upper])
            add_rows(block(half, 3, dg), upper, rf.at[half, dg])
            send(("n", half, dg, "d"), lambda: block(half, 3, dg), lambda: rn.at[half, dg, 1], f + "-")
        elif kind == "total":
            arrived(("n", half, dg, "u"), rn.at[half, dg, 0])
            arrived(("n", half, dg, "d"), rn.at[half, dg, 1])
            ref = block(half, 0, dg)
            sums = ref[...].astype(F32) + rn[half, dg, 0].astype(F32) + rn[half, dg, 1].astype(F32)
            if dg == 0:
                total[half] = sums
            else:
                ref[...] = sums.astype(BF16)
        elif kind == "gfar":
            ref = lambda: block(half, 0, 2)
            send(("g", half, "f0"), lambda: ref().at[lower], lambda: rgf.at[half, lower], g + "+")
            send(("g", half, "f1"), lambda: ref().at[upper], lambda: rgf.at[half, upper], g + "-")
        elif kind == "gup":
            arrived(("g", half, "f0"), rgf.at[half, lower])
            add_rows(block(half, 0, 1), lower, rgf.at[half])
            send(("g", half, "u"), lambda: block(half, 0, 1), lambda: rgn.at[half, 0], g + "+")
        elif kind == "gdown":
            arrived(("g", half, "f1"), rgf.at[half, upper])
            add_rows(block(half, 0, 3), upper, rgf.at[half])
            send(("g", half, "d"), lambda: block(half, 0, 3), lambda: rgn.at[half, 1], g + "-")

    steps = lay_out(unit_of)
    doc_a, doc_b = doc_ref[2 * cp], doc_ref[2 * cp + 1]
    first_a, first_b = first_ref[doc_a], first_ref[doc_b]
    count_a, count_b = count_ref[doc_a], count_ref[doc_b]
    ones = jnp.ones((HD, HD), BF16)
    image_row = lax.broadcasted_iota(jnp.int32, (32, TOK), 0)
    on_a = (image_row == 2 * cp).astype(F32)
    on_b = (image_row == 2 * cp + 1).astype(F32)

    def unit(u, carry):
        j = plus(x, pick(u, [dx for dx, _ in UNITS])) * RING + plus(z, pick(u, [dz for _, dz in UNITS]))
        covers_a = ((first_a <= j) & (j < first_a + count_a)).astype(jnp.int32)
        covers_b = ((first_b <= j) & (j < first_b + count_b)).astype(jnp.int32)
        masks = jnp.concatenate([qall[j, 0, 512:, :], qall[j, 1, 512:, :]], axis=0).astype(F32)
        weigh = on_a * covers_a.astype(F32) + on_b * covers_b.astype(F32)
        weight_row = jnp.sum(masks * weigh, axis=0, keepdims=True)
        diagonal = eye * weight_row
        weight = jnp.dot(diagonal.astype(BF16), ones, preferred_element_type=F32)
        keys, values = kb[covers_b], vb[covers_b]
        for half in (0, 1):
            scores = lax.dot_general(
                qall[j, half, :512, :], keys, (((1,), (1,)), ((), ())), preferred_element_type=F32
            )
            probs = jnp.exp2(scores).astype(BF16)
            both = jnp.dot(probs, values, preferred_element_type=F32)
            denoms = []
            for g in range(4):
                rows = slice(g * TOK, (g + 1) * TOK)
                pb[half, u, rows, :] = (both[rows, :HD] * weight).astype(BF16)
                denoms.append(jnp.sum(both[rows, HD:] * diagonal, axis=0, keepdims=True))
            denoms.append(jnp.zeros((12, TOK), F32))
            pb[half, u, 512:, :] = jnp.concatenate(denoms, axis=0).astype(BF16)
        for at in range(len(UNITS)):
            here = [step for step in steps if step[0] == at]
            if here:
                @pl.when(u == at)
                def _():
                    for _, _, kind, half, dg in here:
                        do(kind, half, dg)
        return carry

    lax.fori_loop(0, len(UNITS), unit, 0)
    for slot, _, kind, half, dg in steps:
        if slot >= len(UNITS):
            do(kind, half, dg)

    for half in (0, 1):
        arrived(("g", half, "u"), rgn.at[half, 0])
        arrived(("g", half, "d"), rgn.at[half, 1])
        sums = total[half] + rgn[half, 0].astype(F32) + rgn[half, 1].astype(F32)
        for g in range(4):
            denom = sums[512 + g : 513 + g, :]
            inv = jnp.where(denom > 0, 1.0 / jnp.where(denom > 0, denom, 1.0), 0.0)
            inv = jnp.transpose(jnp.broadcast_to(inv, (TOK, TOK)))
            cols = slice((half * 4 + g) * HD, (half * 4 + g + 1) * HD)
            out_ref[:, cols] = (sums[g * TOK : (g + 1) * TOK, :] * inv).astype(BF16)

    for k in range(8):
        copy_of(kv_c[k], cs.at[k], cr.at[k], "c").wait_send()
    for key, src, dst, peer in started:
        copy_of(key, src(), dst(), peer).wait_send()


SEMAPHORES = 136


def per_device(
    image_rows, kv_weight, k_gain, tokens, ln_gain, q_weight, q_gain, image_doc, doc_first, doc_count, token_mask
):
    vmem = pl.BlockSpec(memory_space=pltpu.VMEM)
    smem = pl.BlockSpec(memory_space=pltpu.SMEM)
    hbm = pl.BlockSpec(memory_space=pl.ANY)
    width = kv_weight.shape[0]
    cols = q_weight.shape[1]
    scratch = [
        pltpu.VMEM(image_rows.shape, BF16),
        pltpu.VMEM((8, width, 2 * HD), BF16),
        pltpu.VMEM(q_weight.shape, BF16),
        pltpu.VMEM((8,) + tokens.shape, BF16),
        pltpu.VMEM((8, KV_ROWS, 2 * HD), BF16),
        pltpu.VMEM((8, KV_ROWS, 2 * HD), BF16),
        pltpu.VMEM((8, KV_ROWS, 2 * HD), BF16),
        pltpu.VMEM((6, KV_ROWS, 2 * HD), BF16),
        pltpu.VMEM((TOK, cols), F32),
        pltpu.VMEM((SHARDS, 2, HALF, HD), BF16),
        pltpu.VMEM((2, KEYS, HD), BF16),
        pltpu.VMEM((2, KEYS, 2 * HD), BF16),
        pltpu.VMEM((2, SHARDS, HALF, HD), BF16),
        pltpu.VMEM((2, RING, HALF, HD), BF16),
        pltpu.VMEM((2, RING, 2, HALF, HD), BF16),
        pltpu.VMEM((2, HALF, HD), BF16),
        pltpu.VMEM((2, 2, HALF, HD), BF16),
        pltpu.VMEM((2, HALF, HD), F32),
        pltpu.SemaphoreType.DMA((18,)),
        pltpu.SemaphoreType.DMA((SEMAPHORES,)),
        pltpu.SemaphoreType.DMA((SEMAPHORES,)),
    ]
    return pl.pallas_call(
        kernel,
        out_shape=jax.ShapeDtypeStruct((tokens.shape[0], cols), BF16),
        in_specs=[hbm, hbm, vmem, vmem, vmem, hbm, vmem, smem, smem, smem, vmem],
        out_specs=vmem,
        scratch_shapes=scratch,
        compiler_params=pltpu.CompilerParams(
            collective_id=0, has_side_effects=True, vmem_limit_bytes=62 * 2**20
        ),
        name="cross_attention",
    )(
        image_rows, kv_weight, k_gain.reshape(1, HD), tokens, ln_gain.reshape(8, 8, 128), q_weight,
        q_gain.reshape(1, HD), image_doc, doc_first, doc_count, token_mask,
    )


def solution(mesh):
    in_specs = (
        P("cp", None, ("segment", "tp")),
        P(("segment", "tp"), None),
        P(),
        P("cp", ("segment", "tp")),
        P(),
        P(None, ("segment", "tp")),
        P(),
        P(),
        P(),
        P(),
        P("cp", None),
    )
    out_specs = P("cp", ("segment", "tp"))
    return jax.shard_map(
        per_device, mesh=mesh, in_specs=in_specs, out_specs=out_specs, check_vma=False
    )
```

time: 520 us -> 89.3 us (0.17)
  the two profiles are of different devices: /device:TPU:3 before, /device:TPU:0 now
where the time goes in v1:
time: 89.3 us; the launch traced here: 89.1 us
  Pallas kernels  81.3 us (91%)
  local copies, waits for them, and re-layouts  7.73 us (9%)
    pallas_call x1, Pallas kernels, per_device(): pl.pallas_call(kernel, out_shape=jax.ShapeDtypeStruct((tokens.shape[0], c...  81.3 us
    unnamed x3, local copies, waits for them, and re-layouts  7.73 us

profile of v1, /device:TPU:0, one launch (start us, length us, event | category | flops | bytes accessed | tf_op | source)
XLA Modules:
  0.0 89.1 jit_solution(16765613511725108864)
XLA Ops:
  0.0 1.4 %copy.13.mask_ref = s32[128,32]{1,0:T(8,128)} copy(s32[128,32]{0,1:T(8,128)} %param.21) | data formatting | bytes 32768 | tf_op args[10]
  1.4 4.6 %copy.12.x_hbm = bf16[2,801,1024]{2,1,0:T(8,128)(2,1)} copy(bf16[2,801,1024]{2,0,1:T(2,128)(2,1)} %param.11) | data formatting | bytes 6561792 | tf_op args[0]
  6.1 81.3 %cross_attention.1 = bf16[128,1024]{1,0:T(8,128)(2,1)} custom-call(bf16[2,801,1024]{2,1,0:T(8,128)(2,1)} %copy.12.x_hbm, bf16[1024,2048]{1,0:T(8,128)(2,1)} %w_hbm.1, f32[1,128]{1,0:T(1,128)} %bitcast.4, bf16[128,1024]{1,0:T(8,128)(2,1)} %tok_ref.1, f32[8,8,128]{2,1,0:T(8,128)} %bitcast.3, bf16[8192,1024]{1,0:T(8,128)(2,1)} %wq_hbm.1, f32[1,128]{1,0:T(1,128)} %bitcast.5, ...), custom_call_target="tpu_custom_call" | custom-call | tf_op jit(solution)/shard_map/cross_attention/pallas_call | solution.py:479
  87.4 1.7 %copy.15 = bf16[128,1024]{1,0:T(8,128)(2,1)} copy(bf16[128,1024]{1,0:T(8,128)(2,1)} %cross_attention.1) | data formatting | bytes 524288

commit v2 on v1

--- a/solution.py
+++ b/solution.py
@@ -19,6 +19,8 @@
 HD = 128
 IMG_TOK = 801
 KV_ROWS = 816
+KV_CUT = 800
+KV_ALL = 1632
 KEYS = 896
 HALF = 528
 CUT = 256
@@ -64,9 +66,10 @@
 
 
 def kernel(
-    x_hbm, w_hbm, kg_ref, tok_ref, ln_ref, wq_hbm, qg_ref, doc_ref, first_ref, count_ref, mask_ref,
+    x_hbm, w_hbm, kg_hbm, tok_hbm, ln_hbm, wq_hbm, qg_hbm, doc_hbm, first_hbm, count_hbm, mask_hbm,
     out_ref,
-    xs, ws, wq, tok, cs, cr, mine, yr, acc, qall, kb, vb, pb, rf, rn, rgf, rgn, total,
+    kg_ref, tok_ref, ln_ref, qg_ref, doc_ref, first_ref, count_ref, mask_ref,
+    x3, xs, ws, wq, tok, cs, cr, mine, yr, fk, fv, acc, qall, kb, vb, pb, rf, rn, rgf, rgn, total,
     load_sem, send_sem, recv_sem,
 ):
     s = lax.axis_index("segment")
@@ -114,7 +117,11 @@
     def head_cols(head):
         return pl.ds(pl.multiple_of(head * 2 * HD, 2 * HD), 2 * HD)
 
-    x_loads = [load(i, x_hbm.at[i], xs.at[i]) for i in range(2)]
+    first_tok = 416
+    x_loads = [
+        load(0, x_hbm.at[pl.ds(0, first_tok)], x3.at[pl.ds(0, first_tok)]),
+        load(1, x_hbm.at[pl.ds(first_tok, IMG_TOK - first_tok)], x3.at[pl.ds(first_tok, IMG_TOK - first_tok)]),
+    ]
     w_loads = {}
     for at, dt in enumerate((2, 1, 3, 0)):
         for other in (1, 0):
@@ -129,6 +136,15 @@
         load(10 + n, wq_hbm.at[pl.ds(pl.multiple_of(b * width, width), width)], wq.at[pl.ds(n * width, width)])
         for n, b in enumerate(blocks)
     ]
+    small_loads = [
+        load(18 + n, src, dst)
+        for n, (src, dst) in enumerate(
+            ((tok_hbm, tok_ref), (ln_hbm, ln_ref), (qg_hbm, qg_ref), (mask_hbm, mask_ref),
+             (kg_hbm, kg_ref), (doc_hbm, doc_ref), (first_hbm, first_ref), (count_hbm, count_ref))
+        )
+    ]
+    for copy in small_loads:
+        copy.start()
     x_loads[0].start()
     w_loads[2, 1].start()
     w_loads[2, 0].start()
@@ -136,40 +152,54 @@
     for dt in (1, 3, 0):
         w_loads[dt, 1].start()
         w_loads[dt, 0].start()
-    for copy in wq_loads:
-        copy.start()
 
     barrier = pltpu.get_barrier_semaphore()
     for peer in peers.values():
         pl.semaphore_signal(barrier, inc=1, device_id=peer, device_id_type=MESH)
 
+    small_loads[0].wait()
+    small_loads[1].wait()
     gain = ln_ref[s * RING + t]
     for c in range(8):
         cols = slice(c * 128, (c + 1) * 128)
         tok[0, :, cols] = (tok_ref[:, cols].astype(F32) * gain[c : c + 1, :]).astype(BF16)
+    for copy in small_loads[2:]:
+        copy.wait()
     pl.semaphore_wait(barrier, len(peers))
 
     send(("tok", "y+"), lambda: tok.at[0], lambda: tok.at[2], "y+")
     send(("tok", "y-"), lambda: tok.at[0], lambda: tok.at[3], "y-")
     send(("tok", "c0"), lambda: tok.at[0], lambda: tok.at[1], "c")
 
-    cut = 400
     kv_c = [number(("kvc", k)) for k in range(8)]
-    assert kv_c == list(range(kv_c[0], kv_c[0] + 8))
+
+    def interleave(lo, hi):
+        def step(n, carry):
+            rows = pl.ds(pl.multiple_of(n * 32, 32), 32)
+            xs[rows, :] = x3[pl.ds(pl.multiple_of(n * 16, 16), 16)].reshape(32, x3.shape[2])
+            return carry
+
+        lax.fori_loop(lo, hi, step, 0)
 
     def kv_slot(k, carry):
         dt_at = pick(k, [(2, 1, 3, 0).index(dt) for dt, _ in KV_ORDER])
-        img = pick(k, [i for _, i in KV_ORDER])
+        half = pick(k, [h for _, h in KV_ORDER])
 
         @pl.when(k == 0)
         def _():
             x_loads[0].wait()
+            interleave(0, first_tok // 16)
             w_loads[2, 1].wait()
             w_loads[2, 0].wait()
 
         @pl.when(k == 1)
         def _():
             x_loads[1].wait()
+            for copy in wq_loads:
+                copy.start()
+            interleave(first_tok // 16, 50)
+            last = x3[IMG_TOK - 1 : IMG_TOK].reshape(2, x3.shape[2])
+            xs[2 * IMG_TOK - 2 :, :] = jnp.concatenate([last, jnp.zeros((14, x3.shape[2]), BF16)], axis=0)
 
         for first_use, dt in ((2, 1), (3, 3), (6, 0)):
             @pl.when(k == first_use)
@@ -177,23 +207,32 @@
                 w_loads[dt, 1].wait()
                 w_loads[dt, 0].wait()
 
+        rows = pl.ds(pl.multiple_of(half * KV_CUT, 32), KV_ROWS)
         for which, dst in ((0, cs), (1, mine)):
-            dst[k, 800:, :] = jnp.zeros((KV_ROWS - 800, 2 * HD), BF16)
-            weight = ws[dt_at * 2 + which]
-            for lo, hi in ((0, cut), (cut, IMG_TOK)):
-                dst[k, lo:hi, :] = jnp.dot(xs[img, lo:hi, :], weight, preferred_element_type=F32).astype(BF16)
+            dst[k] = jnp.dot(xs[rows, :], ws[dt_at * 2 + which], preferred_element_type=F32).astype(BF16)
             if which == 0:
                 copy_of(kv_c[0] + k, cs.at[k], cr.at[k], "c").start()
 
-        @pl.when(k > 0)
+        @pl.when(k > 1)
         def _():
-            before = k - 1
-            arrived(kv_c[0] + before, cr.at[before])
-            mine[before] = (mine[before].astype(F32) + cr[before].astype(F32)).astype(BF16)
+            add_other(k - 2)
 
         return carry
 
-    lax.fori_loop(0, 5, kv_slot, 0)
+    def add_other(k):
+        arrived(kv_c[0] + k, cr.at[k])
+        mine[k] = mine[k] + cr[k]
+
+    halves = (pl.ds(0, KV_CUT), pl.ds(0, KV_ROWS))
+
+    def send_kv(tag, k, to, peer):
+        rows = halves[KV_ORDER[k][1]]
+        send(("kv",) + tag, lambda: mine.at[k, rows], lambda: yr.at[to, rows], peer)
+
+    def kv_arrived(tag, to, half):
+        arrived(("kv",) + tag, yr.at[to, halves[half]])
+
+    lax.fori_loop(0, 4, kv_slot, 0)
 
     half_tok = TOK // 2
     arrived(("tok", "y+"), tok.at[2])
@@ -203,12 +242,9 @@
     send(("tokf", "y-"), lambda: tok.at[3, half_tok:], lambda: tok.at[6, half_tok:], "y-")
     send(("tok", "c3"), lambda: tok.at[3], lambda: tok.at[5], "c")
 
-    lax.fori_loop(5, 8, kv_slot, 0)
-
-    send(("kv", "far", 0), lambda: mine.at[0], lambda: yr.at[0], "y+")
-    send(("kv", "far", 1), lambda: mine.at[1], lambda: yr.at[1], "y-")
-    arrived(kv_c[7], cr.at[7])
-    mine[7] = (mine[7].astype(F32) + cr[7].astype(F32)).astype(BF16)
+    lax.fori_loop(4, 5, kv_slot, 0)
+    send_kv(("far", 0), 0, 0, "y+")
+    send_kv(("far", 1), 1, 1, "y-")
 
     arrived(("tok", "c0"), tok.at[1])
     arrived(("tok", "c2"), tok.at[4])
@@ -226,11 +262,12 @@
         return carry
 
     lax.fori_loop(0, 6, project, 0)
-    send(("kv", "near", 1, 1), lambda: mine.at[2], lambda: yr.at[3], "y+")
-    send(("kv", "near", 3, 0), lambda: mine.at[3], lambda: yr.at[4], "y-")
     arrived(("tokf", "y+"), tok.at[6, 0:half_tok])
     arrived(("tokf", "y-"), tok.at[6, half_tok:])
     send(("tok", "c6"), lambda: tok.at[6], lambda: tok.at[7], "c")
+    lax.fori_loop(5, 6, kv_slot, 0)
+    send_kv(("near", 1, 1), 2, 3, "y+")
+    send_kv(("near", 3, 0), 3, 4, "y-")
     arrived(("tok", "c6"), tok.at[7])
     lax.fori_loop(6, 8, project, 0)
 
@@ -242,10 +279,7 @@
         raw = acc[:, g * HD : (g + 1) * HD]
         inv = lax.rsqrt(jnp.mean(raw * raw, axis=-1, keepdims=True) + EPSILON)
         qall[cp, g // 4, (g % 4) * TOK : (g % 4 + 1) * TOK, :] = (raw * inv * q_scale).astype(BF16)
-    eye_img = eye[:32, :32].astype(BF16)
-    mask_rows = lax.dot_general(
-        eye_img, mask_ref[...].astype(F32).astype(BF16), (((1,), (1,)), ((), ())), preferred_element_type=F32
-    )
+    mask_rows = mask_ref[...].astype(F32)
     for half in (0, 1):
         qall[cp, half, 512:, :] = mask_rows[half * 16 : (half + 1) * 16, :].astype(BF16)
 
@@ -273,12 +307,20 @@
         forward(("b", 0, 0), half, cp, b + "+")
         forward(("b", 0, 1), half, cp, b + "-")
 
-    arrived(("kv", "far", 0), yr.at[0])
-    mine[4] = (mine[4].astype(F32) + yr[0].astype(F32)).astype(BF16)
-    send(("kv", "near", 1, 0), lambda: mine.at[4], lambda: yr.at[2], "y+")
-    arrived(("kv", "far", 1), yr.at[1])
-    mine[5] = (mine[5].astype(F32) + yr[1].astype(F32)).astype(BF16)
-    send(("kv", "near", 3, 1), lambda: mine.at[5], lambda: yr.at[5], "y-")
+    lax.fori_loop(6, 8, kv_slot, 0)
+    add_other(6)
+    add_other(7)
+
+    def add_passing(k, to):
+        rows = halves[KV_ORDER[k][1]]
+        mine[k, rows, :] = mine[k, rows, :] + yr[to, rows, :]
+
+    kv_arrived(("far", 0), 0, 0)
+    add_passing(4, 0)
+    send_kv(("near", 1, 0), 4, 2, "y+")
+    kv_arrived(("far", 1), 1, 1)
+    add_passing(5, 1)
+    send_kv(("near", 3, 1), 5, 5, "y-")
 
     for half in (0, 1):
         a, b = axes[half]
@@ -316,18 +358,25 @@
         kb[img, KV_ROWS:, :] = jnp.zeros((KEYS - KV_ROWS, HD), BF16)
         vb[img, KV_ROWS:, :] = jnp.zeros((KEYS - KV_ROWS, 2 * HD), BF16)
         vb[img, :KV_ROWS, HD:] = jnp.where(live, 1.0, 0.0).astype(BF16)
-    for img in (1, 0):
-        arrived(("kv", "near", 1, img), yr.at[2 + img])
-        arrived(("kv", "near", 3, img), yr.at[4 + img])
-        keys = (
-            mine[6 + img, :, :HD].astype(F32) + yr[2 + img, :, :HD].astype(F32) + yr[4 + img, :, :HD].astype(F32)
-        )
+    fk[KV_CUT + KV_ROWS :, :] = jnp.zeros((KV_ALL - KV_CUT - KV_ROWS, HD), F32)
+    fv[KV_CUT + KV_ROWS :, :] = jnp.zeros((KV_ALL - KV_CUT - KV_ROWS, HD), F32)
+    for half in (0, 1):
+        kv_arrived(("near", 1, half), 2 + half, half)
+        kv_arrived(("near", 3, half), 4 + half, half)
+        rows = halves[half]
+        to = pl.ds(half * KV_CUT, rows.size)
+        for ref, cols in ((fk, slice(0, HD)), (fv, slice(HD, 2 * HD))):
+            ref[to, :] = (
+                mine[6 + half, rows, cols].astype(F32)
+                + yr[2 + half, rows, cols].astype(F32)
+                + yr[4 + half, rows, cols].astype(F32)
+            )
+    for img in (0, 1):
+        every = pl.ds(img, KV_ROWS, stride=2)
+        keys = fk[every, :]
         inv = lax.rsqrt(jnp.mean(keys * keys, axis=-1, keepdims=True) + EPSILON)
         kb[img, :KV_ROWS, :] = jnp.where(live, keys * inv * kg_ref[...], 0.0).astype(BF16)
-        values = (
-            mine[6 + img, :, HD:].astype(F32) + yr[2 + img, :, HD:].astype(F32) + yr[4 + img, :, HD:].astype(F32)
-        )
-        vb[img, :KV_ROWS, :HD] = jnp.where(live, values, 0.0).astype(BF16)
+        vb[img, :KV_ROWS, :HD] = jnp.where(live, fv[every, :], 0.0).astype(BF16)
 
     for da in (0, 3, 1, 2):
         for half in (0, 1):
@@ -341,7 +390,7 @@
         return pb.at[half, unit_of[(dg, df) if half == 0 else (df, dg)]]
 
     def add_rows(ref, rows, other):
-        ref[rows, :] = (ref[rows, :].astype(F32) + other[rows, :].astype(F32)).astype(BF16)
+        ref[rows, :] = ref[rows, :] + other[rows, :]
 
     def do(kind, half, dg):
         f, g = rs_axes[half]
@@ -449,12 +498,21 @@
     image_rows, kv_weight, k_gain, tokens, ln_gain, q_weight, q_gain, image_doc, doc_first, doc_count, token_mask
 ):
     vmem = pl.BlockSpec(memory_space=pltpu.VMEM)
-    smem = pl.BlockSpec(memory_space=pltpu.SMEM)
     hbm = pl.BlockSpec(memory_space=pl.ANY)
     width = kv_weight.shape[0]
     cols = q_weight.shape[1]
+    rows = jnp.transpose(image_rows, (1, 0, 2))
     scratch = [
-        pltpu.VMEM(image_rows.shape, BF16),
+        pltpu.VMEM((1, HD), F32),
+        pltpu.VMEM(tokens.shape, BF16),
+        pltpu.VMEM((8, 8, 128), F32),
+        pltpu.VMEM((1, HD), F32),
+        pltpu.SMEM(image_doc.shape, jnp.int32),
+        pltpu.SMEM(doc_first.shape, jnp.int32),
+        pltpu.SMEM(doc_count.shape, jnp.int32),
+        pltpu.VMEM((32, TOK), jnp.int32),
+        pltpu.VMEM(rows.shape, BF16),
+        pltpu.VMEM((KV_CUT + KV_ROWS, width), BF16),
         pltpu.VMEM((8, width, 2 * HD), BF16),
         pltpu.VMEM(q_weight.shape, BF16),
         pltpu.VMEM((8,) + tokens.shape, BF16),
@@ -462,6 +520,8 @@
         pltpu.VMEM((8, KV_ROWS, 2 * HD), BF16),
         pltpu.VMEM((8, KV_ROWS, 2 * HD), BF16),
         pltpu.VMEM((6, KV_ROWS, 2 * HD), BF16),
+        pltpu.VMEM((KV_ALL, HD), F32),
+        pltpu.VMEM((KV_ALL, HD), F32),
         pltpu.VMEM((TOK, cols), F32),
         pltpu.VMEM((SHARDS, 2, HALF, HD), BF16),
         pltpu.VMEM((2, KEYS, HD), BF16),
@@ -472,14 +532,14 @@
         pltpu.VMEM((2, HALF, HD), BF16),
         pltpu.VMEM((2, 2, HALF, HD), BF16),
         pltpu.VMEM((2, HALF, HD), F32),
-        pltpu.SemaphoreType.DMA((18,)),
+        pltpu.SemaphoreType.DMA((26,)),
         pltpu.SemaphoreType.DMA((SEMAPHORES,)),
         pltpu.SemaphoreType.DMA((SEMAPHORES,)),
     ]
     return pl.pallas_call(
         kernel,
         out_shape=jax.ShapeDtypeStruct((tokens.shape[0], cols), BF16),
-        in_specs=[hbm, hbm, vmem, vmem, vmem, hbm, vmem, smem, smem, smem, vmem],
+        in_specs=[hbm] * 11,
         out_specs=vmem,
         scratch_shapes=scratch,
         compiler_params=pltpu.CompilerParams(
@@ -487,8 +547,8 @@
         ),
         name="cross_attention",
     )(
-        image_rows, kv_weight, k_gain.reshape(1, HD), tokens, ln_gain.reshape(8, 8, 128), q_weight,
-        q_gain.reshape(1, HD), image_doc, doc_first, doc_count, token_mask,
+        rows, kv_weight, k_gain.reshape(1, HD), tokens, ln_gain.reshape(8, 8, 128), q_weight,
+        q_gain.reshape(1, HD), image_doc, doc_first, doc_count, token_mask.T,
     )
 
 

time: 89.3 us -> 82.2 us (0.920)
  local copies, waits for them, and re-layouts: 7.73 us -> 1.67 us
  Pallas kernels: 81.3 us -> 80.4 us
    unnamed x3 -> x1, local copies, waits for them, and re-layouts: 7.73 us -> 1.67 us
    pallas_call x1, Pallas kernels: 81.3 us -> 80.4 us  [per_device(): pl.pallas_call(kernel, out_shape=jax.ShapeDtypeStruct((tokens.shape[0], c...]
where the time goes in v2:
time: 82.2 us; the launch traced here: 82.1 us
  Pallas kernels  80.4 us (98%)
  local copies, waits for them, and re-layouts  1.67 us (2%)
    pallas_call x1, Pallas kernels, per_device(): pl.pallas_call(kernel, out_shape=jax.ShapeDtypeStruct((tokens.shape[0], c...  80.4 us
    unnamed x1, local copies, waits for them, and re-layouts  1.67 us

profile of v2, /device:TPU:0, one launch (start us, length us, event | category | flops | bytes accessed | tf_op | source)
XLA Modules:
  0.0 82.1 jit_solution(17257692905909948666)
XLA Ops:
  0.0 80.4 %cross_attention.1 = bf16[128,1024]{1,0:T(8,128)(2,1)} custom-call(bf16[801,2,1024]{2,1,0:T(2,128)(2,1)} %bitcast.5, bf16[1024,2048]{1,0:T(8,128)(2,1)} %w_hbm.1, f32[1,128]{1,0:T(1,128)} %bitcast.8, bf16[128,1024]{1,0:T(8,128)(2,1)} %tok_hbm.1, f32[8,8,128]{2,1,0:T(8,128)} %bitcast.6, bf16[8192,1024]{1,0:T(8,128)(2,1)} %wq_hbm.1, f32[1,128]{1,0:T(1,128)} %bitcast.9, ...), custom_call_target="tpu_custom_call" | custom-call | tf_op jit(solution)/shard_map/cross_attention/pallas_call | solution.py:539
  80.4 1.7 %copy.13 = bf16[128,1024]{1,0:T(8,128)(2,1)} copy(bf16[128,1024]{1,0:T(8,128)(2,1)} %cross_attention.1) | data formatting | bytes 524288

commit v3 on v0

v3 whole, which is shorter than its diff:
```python
import math

import jax
import jax.numpy as jnp
from jax import lax
from jax.experimental import pallas as pl
from jax.experimental.pallas import tpu as pltpu
from jax.sharding import PartitionSpec as P

EPSILON = 1e-06
MESH = pl.DeviceIdType.MESH
BF16 = jnp.bfloat16
F32 = jnp.float32

RING = 4
TOK = 128
HD = 128
IMG_TOK = 801
IMG_ROWS = 1616
KEYS = 896
HALF = 528


class Chunk:
    def __init__(self, key, keys, sent):
        self.key, self.keys = key, keys
        self.sent = sent
        self.row = 2 * key
        end = min(2 * (key + sent), IMG_ROWS)
        self.half = (end - self.row) // 32 * 16
        self.rows = end - self.row - self.half
        self.halves = (pl.ds(0, self.half), pl.ds(0, self.rows))


CHUNKS = (Chunk(0, 512, 512), Chunk(512, 384, 304))
KV_ORDER = ((2, 0), (2, 1), (1, 1), (3, 0), (1, 0), (3, 1), (0, 0), (0, 1))
SOURCES = (0, 3, 1, 2)
EARLY = 6
TARGETS = (2, 1, 3, 0)


def pick(index, values):
    return sum((index == at).astype(jnp.int32) * value for at, value in enumerate(values) if value)


def kernel(
    x_hbm, w_hbm, kg_hbm, tok_hbm, ln_hbm, wq_hbm, qg_hbm, doc_hbm, first_hbm, count_hbm, mask_hbm,
    out_ref,
    kg_ref, tok_ref, ln_ref, qg_ref, doc_ref, first_ref, count_ref, mask_ref,
    x3, xs, ws, wq, tok, fk, fv, acc, qall, weights, kvb, oacc, pb, rn,
    load_sem, send_sem, recv_sem,
    *kv_refs,
):
    s = lax.axis_index("segment")
    cp = lax.axis_index("cp")
    t = lax.axis_index("tp")
    x, z = cp // RING, cp % RING

    def plus(v, n):
        return lax.rem(v + n, RING)

    a, b = z * (1 - s) + x * s, x * (1 - s) + z * s

    def shard(da, db):
        at_a, at_b = plus(a, da), plus(b, db)
        return (at_b * (1 - s) + at_a * s) * RING + at_a * (1 - s) + at_b * s

    peers = {
        "c": (1 - s, cp, t),
        "y+": (s, cp, plus(t, 1)),
        "y-": (s, cp, plus(t, 3)),
        "a+": (s, shard(1, 0), t),
        "a-": (s, shard(3, 0), t),
        "b+": (s, shard(0, 1), t),
        "b-": (s, shard(0, 3), t),
        "a2": (s, shard(2, 0), t),
        "b2": (s, shard(0, 2), t),
    }

    numbers = {}

    def number(key):
        return numbers.setdefault(key, len(numbers))

    started = {}

    def copy_of(key, src, dst, peer):
        n = number(key) if isinstance(key, tuple) else key
        return pltpu.make_async_remote_copy(
            src_ref=src, dst_ref=dst, send_sem=send_sem.at[n], recv_sem=recv_sem.at[n],
            device_id=peers[peer], device_id_type=MESH,
        )

    def send(key, src, dst, peer):
        copy_of(key, src(), dst(), peer).start()
        started[key] = (src, dst, peer)

    def arrived(key, dst):
        copy_of(key, dst, dst, "c").wait_recv()

    def load(n, src, dst):
        return pltpu.make_async_copy(src, dst, load_sem.at[n])

    def head_cols(head):
        return pl.ds(pl.multiple_of(head * 2 * HD, 2 * HD), 2 * HD)

    first_tok = CHUNKS[0].sent
    x_loads = [
        load(0, x_hbm.at[pl.ds(0, first_tok)], x3.at[pl.ds(0, first_tok)]),
        load(1, x_hbm.at[pl.ds(first_tok, IMG_TOK - first_tok)], x3.at[pl.ds(first_tok, IMG_TOK - first_tok)]),
    ]
    w_loads = {}
    for at, dt in enumerate((2, 1, 3, 0)):
        for other in (1, 0):
            head = (1 - s if other else s) * RING + plus(t, dt)
            w_loads[dt, other] = load(
                2 + at * 2 + (1 - other), w_hbm.at[:, head_cols(head)], ws.at[at * 2 + (1 - other)]
            )
    tok_order = ((0, 0), (1, 0), (0, 3), (0, 1), (1, 3), (1, 1), (0, 2), (1, 2))
    blocks = [(1 - s if o else s) * RING + plus(t, dt) for o, dt in tok_order]
    width = wq.shape[0] // 8
    wq_loads = [
        load(10 + n, wq_hbm.at[pl.ds(pl.multiple_of(b * width, width), width)], wq.at[pl.ds(n * width, width)])
        for n, b in enumerate(blocks)
    ]
    small_loads = [
        load(18 + n, src, dst)
        for n, (src, dst) in enumerate(
            ((tok_hbm, tok_ref), (ln_hbm, ln_ref), (qg_hbm, qg_ref), (mask_hbm, mask_ref),
             (kg_hbm, kg_ref), (doc_hbm, doc_ref), (first_hbm, first_ref), (count_hbm, count_ref))
        )
    ]
    for copy in small_loads:
        copy.start()
    x_loads[0].start()
    w_loads[2, 1].start()
    w_loads[2, 0].start()
    x_loads[1].start()
    for dt in (1, 3, 0):
        w_loads[dt, 1].start()
        w_loads[dt, 0].start()

    barrier = pltpu.get_barrier_semaphore()
    for peer in peers.values():
        pl.semaphore_signal(barrier, inc=1, device_id=peer, device_id_type=MESH)

    small_loads[0].wait()
    small_loads[1].wait()
    gain = ln_ref[s * RING + t]
    for c in range(8):
        cols = slice(c * 128, (c + 1) * 128)
        tok[0, :, cols] = (tok_ref[:, cols].astype(F32) * gain[c : c + 1, :]).astype(BF16)
    for copy in small_loads[2:]:
        copy.wait()
    pl.semaphore_wait(barrier, len(peers))

    half_tok = TOK // 2
    tok_half = (slice(0, half_tok), slice(half_tok, TOK))

    def send_tok(tag, half, src, dst, peer):
        send(("tok",) + tag + (half,), lambda: tok.at[src, tok_half[half]], lambda: tok.at[dst, tok_half[half]], peer)

    def tok_arrived(tag, half, at):
        arrived(("tok",) + tag + (half,), tok.at[at, tok_half[half]])

    for first in (0, 1):
        send_tok(("y+",), first, 0, 2, "y+")
        send_tok(("y-",), 1 - first, 0, 3, "y-")
    send(("tok", "c0"), lambda: tok.at[0], lambda: tok.at[1], "c")

    n_chunks = len(CHUNKS)
    cs, cr, mine, yr = (kv_refs[n * n_chunks : (n + 1) * n_chunks] for n in range(4))
    kv_c = [[number(("kvc", c, k)) for k in range(8)][0] for c in range(n_chunks)]

    def interleave(lo, hi):
        def step(n, carry):
            rows = pl.ds(pl.multiple_of(n * 32, 32), 32)
            xs[rows, :] = x3[pl.ds(pl.multiple_of(n * 16, 16), 16)].reshape(32, x3.shape[2])
            return carry

        lax.fori_loop(lo, hi, step, 0)

    def kv_slots(c, which, lo, hi):
        chunk = CHUNKS[c]

        def kv_slot(k, carry):
            dt_at = pick(k, [(2, 1, 3, 0).index(dt) for dt, _ in KV_ORDER])
            half = pick(k, [h for _, h in KV_ORDER])
            for first_use, dt in ((0, 2), (2, 1), (3, 3), (6, 0)):
                if c == 0 and lo <= first_use < hi:
                    @pl.when(k == first_use)
                    def _():
                        w_loads[dt, 1 - which].wait()

            rows = pl.ds(pl.multiple_of(chunk.row + half * chunk.half, 16), chunk.rows)
            part = jnp.dot(xs[rows, :], ws[dt_at * 2 + which], preferred_element_type=F32).astype(BF16)
            if which == 0:
                cs[c][k] = part
                copy_of(kv_c[c] + k, cs[c].at[k], cr[c].at[k], "c").start()
            else:
                arrived(kv_c[c] + k, cr[c].at[k])
                mine[c][k] = part + cr[c][k]
            return carry

        lax.fori_loop(lo, hi, kv_slot, 0)

    OTHER, MINE = 0, 1

    def send_kv(c, tag, k, to, peer):
        rows = CHUNKS[c].halves[KV_ORDER[k][1]]
        send(("kv", c) + tag, lambda: mine[c].at[k, rows], lambda: yr[c].at[to, rows], peer)

    def kv_arrived(c, tag, to, half):
        arrived(("kv", c) + tag, yr[c].at[to, CHUNKS[c].halves[half]])

    def kv_far(c):
        send_kv(c, ("far", 0), 0, 0, "y+")
        send_kv(c, ("far", 1), 1, 1, "y-")

    def kv_near(c):
        send_kv(c, ("near", 1, 1), 2, 3, "y+")
        send_kv(c, ("near", 3, 0), 3, 4, "y-")

    def kv_pass(c):
        for half, k, tag, peer in ((0, 4, ("near", 1, 0), "y+"), (1, 5, ("near", 3, 1), "y-")):
            rows = CHUNKS[c].halves[half]
            kv_arrived(c, ("far", half), half, half)
            mine[c][k, rows, :] = mine[c][k, rows, :] + yr[c][half, rows, :]
            send_kv(c, tag, k, 2 if half == 0 else 5, peer)

    x_loads[0].wait()
    interleave(0, first_tok // 16)
    kv_slots(0, OTHER, 0, 6)
    x_loads[1].wait()
    for copy in wq_loads:
        copy.start()
    kv_slots(0, MINE, 0, 6)

    tok_arrived(("y+",), 0, 2)
    send_tok(("f+",), 0, 2, 6, "y+")
    tok_arrived(("y-",), 1, 3)
    send_tok(("f-",), 1, 3, 6, "y-")
    tok_arrived(("y+",), 1, 2)
    send(("tok", "c2"), lambda: tok.at[2], lambda: tok.at[4], "c")
    tok_arrived(("y-",), 0, 3)
    send(("tok", "c3"), lambda: tok.at[3], lambda: tok.at[5], "c")
    kv_far(0)

    kv_slots(0, OTHER, 6, 8)
    interleave(first_tok // 16, 50)
    last = x3[IMG_TOK - 1 : IMG_TOK].reshape(2, x3.shape[2])
    xs[2 * IMG_TOK - 2 :, :] = jnp.concatenate([last, jnp.zeros((IMG_ROWS - 2 * IMG_TOK, x3.shape[2]), BF16)], axis=0)
    for c in range(1, n_chunks):
        kv_slots(c, OTHER, 0, 8)

    arrived(("tok", "c0"), tok.at[1])
    arrived(("tok", "c2"), tok.at[4])
    arrived(("tok", "c3"), tok.at[5])
    acc[...] = jnp.zeros_like(acc)

    def project(n, carry):
        for m in range(8):
            @pl.when(n == m)
            def _():
                wq_loads[m].wait()

        rows = pl.ds(pl.multiple_of(n * width, width), width)
        acc[...] += jnp.dot(tok[n], wq[rows, :], preferred_element_type=F32)
        return carry

    lax.fori_loop(0, 6, project, 0)
    kv_near(0)
    tok_arrived(("f+",), 0, 6)
    send_tok(("c6",), 0, 6, 7, "c")
    tok_arrived(("f-",), 1, 6)
    send_tok(("c6",), 1, 6, 7, "c")
    kv_slots(1, MINE, 0, 6)
    tok_arrived(("c6",), 0, 7)
    tok_arrived(("c6",), 1, 7)
    lax.fori_loop(6, 8, project, 0)

    eye = (
        lax.broadcasted_iota(jnp.int32, (HD, HD), 0) == lax.broadcasted_iota(jnp.int32, (HD, HD), 1)
    ).astype(F32)
    q_scale = qg_ref[...] * (math.log2(math.e) / math.sqrt(HD))
    for g in range(8):
        raw = acc[:, g * HD : (g + 1) * HD]
        inv = lax.rsqrt(jnp.mean(raw * raw, axis=-1, keepdims=True) + EPSILON)
        qall[0, g // 4, (g % 4) * TOK : (g % 4 + 1) * TOK, :] = (raw * inv * q_scale).astype(BF16)
    mask_rows = mask_ref[...].astype(F32)
    for half in (0, 1):
        qall[0, half, 512:, :] = mask_rows[half * 16 : (half + 1) * 16, :].astype(BF16)

    ways = (("+", 3), ("-", 1), ("2", 2))
    for way, at in ways:
        send(("q", way), lambda: qall.at[0], lambda at=at: qall.at[at], "b" + way)

    kv_slots(0, MINE, 6, 8)
    kv_pass(0)
    kv_far(1)
    kv_near(1)
    kv_slots(1, MINE, 6, 8)

    tail = CHUNKS[-1].key + CHUNKS[-1].sent
    kvb[:, :, tail:, :] = jnp.zeros((RING, 2, KEYS - tail, 3 * HD), BF16)
    for chunk in CHUNKS:
        index = chunk.key + lax.broadcasted_iota(jnp.int32, (chunk.sent, HD), 0)
        ones_rows = jnp.where(index < IMG_TOK, 1.0, 0.0).astype(BF16)
        for da in range(RING):
            for img in (0, 1):
                kvb[da, img, chunk.key : chunk.key + chunk.sent, 2 * HD :] = ones_rows
    oacc[...] = jnp.zeros_like(oacc)
    fk[IMG_ROWS:, :] = jnp.zeros((16, HD), F32)
    fv[IMG_ROWS:, :] = jnp.zeros((16, HD), F32)

    def kv_ref(c, da):
        return kvb.at[da, :, pl.ds(CHUNKS[c].key, CHUNKS[c].sent), 0 : 2 * HD]

    def kv_finish(c):
        chunk = CHUNKS[c]
        for half in (0, 1):
            kv_arrived(c, ("near", 1, half), 2 + half, half)
            kv_arrived(c, ("near", 3, half), 4 + half, half)
            rows = chunk.halves[half]
            to = pl.ds(chunk.row + half * chunk.half, rows.size)
            for ref, cols in ((fk, slice(0, HD)), (fv, slice(HD, 2 * HD))):
                ref[to, :] = (
                    mine[c][6 + half, rows, cols].astype(F32)
                    + yr[c][2 + half, rows, cols].astype(F32)
                    + yr[c][4 + half, rows, cols].astype(F32)
                )
        live = chunk.key + lax.broadcasted_iota(jnp.int32, (chunk.sent, HD), 0) < IMG_TOK
        for img in (0, 1):
            every = pl.ds(chunk.row + img, chunk.sent, stride=2)
            rows = slice(chunk.key, chunk.key + chunk.sent)
            keys = fk[every, :]
            inv = lax.rsqrt(jnp.mean(keys * keys, axis=-1, keepdims=True) + EPSILON)
            kvb[0, img, rows, 0:HD] = jnp.where(live, keys * inv * kg_ref[...], 0.0).astype(BF16)
            kvb[0, img, rows, HD : 2 * HD] = jnp.where(live, fv[every, :], 0.0).astype(BF16)
        for way, at in ways[: 2 if c == 0 else 3]:
            send(("kva", c, way), lambda: kv_ref(c, 0), lambda at=at: kv_ref(c, at), "a" + way)

    def kv_gathered(c, way):
        at = dict(ways)[way]
        arrived(("kva", c, way), kv_ref(c, at))

    def kv_forward(img, way):
        at = dict(ways)[way]
        kv_gathered(0, way)
        send(("kvf", way), lambda: kv_ref(0, at).at[img], lambda: kv_ref(0, 2).at[img], "a" + way)

    def kv_forwarded():
        for img, way in ((0, "+"), (1, "-")):
            arrived(("kvf", way), kv_ref(0, 2).at[img])

    def settle(db):
        for half in (0, 1):
            pb[db, half, :512, :] = oacc[db, half * 512 : (half + 1) * 512, :HD].astype(BF16)
            denoms = [
                jnp.sum(oacc[db, half * 512 + g * TOK : half * 512 + (g + 1) * TOK, HD:] * eye, axis=0, keepdims=True)
                for g in range(4)
            ]
            pb[db, half, 512:, :] = jnp.concatenate(denoms + [jnp.zeros((12, TOK), F32)], axis=0).astype(BF16)

    def hand_over(db, way, at):
        settle(db)
        send(("n", way), lambda: pb.at[db], lambda: rn.at[at], "b" + way)

    ones = jnp.ones((HD, HD), BF16)
    image_row = lax.broadcasted_iota(jnp.int32, (32, TOK), 0)

    def covered(img, dst):
        doc = doc_ref[img]
        first = first_ref[doc]
        return ((first <= dst) & (dst < first + count_ref[doc])).astype(jnp.int32)

    def weigh(u, carry):
        da, db = lax.div(u, RING), lax.rem(u, RING)
        src, dst = shard(da, 0), shard(0, db)
        masks = jnp.concatenate([qall[db, 0, 512:, :], qall[db, 1, 512:, :]], axis=0).astype(F32)
        chosen = (image_row == 2 * src).astype(F32) * covered(2 * src, dst).astype(F32) + (
            image_row == 2 * src + 1
        ).astype(F32) * covered(2 * src + 1, dst).astype(F32)
        diagonal = eye * jnp.sum(masks * chosen, axis=0, keepdims=True)
        weights[da, db] = jnp.dot(diagonal.astype(BF16), ones, preferred_element_type=F32)
        return carry

    def attend(c, before, by_source):
        chunk = CHUNKS[c]
        rows = pl.ds(chunk.key, chunk.keys)

        def unit(u, carry):
            for at, events in before.items():
                @pl.when(u == at)
                def _():
                    for event in events:
                        event()
            outer, inner = lax.div(u, RING), lax.rem(u, RING)
            da, db = pick(outer if by_source else inner, SOURCES), pick(inner if by_source else outer, TARGETS)
            src, dst = shard(da, 0), shard(0, db)
            second = covered(2 * src + 1, dst)
            weight = weights[da, db]
            picked = jnp.where(second > 0, kvb[da, 1, rows, 0 : 2 * HD], kvb[da, 0, rows, 0 : 2 * HD])
            keys = picked[:, :HD]
            values = jnp.concatenate([picked[:, HD:], kvb[da, 0, rows, 2 * HD :]], axis=1)
            for half in (0, 1):
                scores = lax.dot_general(
                    qall[db, half, :512, :], keys, (((1,), (1,)), ((), ())), preferred_element_type=F32
                )
                both = jnp.dot(jnp.exp2(scores).astype(BF16), values, preferred_element_type=F32)
                for g in range(4):
                    to = slice(half * 512 + g * TOK, half * 512 + (g + 1) * TOK)
                    for cols in (slice(0, HD), slice(HD, 2 * HD)):
                        oacc[db, to, cols] += both[g * TOK : (g + 1) * TOK, cols] * weight
            return carry

        lax.fori_loop(0, RING * RING, unit, 0)

    for way, at in ways:
        arrived(("q", way), qall.at[at])
    lax.fori_loop(0, RING * RING, weigh, 0)
    kv_finish(0)
    attend(
        0,
        {
            3: [lambda: kv_pass(1)],
            4: [lambda: kv_forward(0, "+"), lambda: kv_forward(1, "-")],
            EARLY: [lambda: kv_finish(1)],
            12: [kv_forwarded],
        },
        True,
    )
    attend(
        1,
        {
            1: [lambda: kv_gathered(1, "+")],
            2: [lambda: kv_gathered(1, "-")],
            3: [lambda: kv_gathered(1, "2")],
            4: [lambda: hand_over(2, "2", 2)],
            8: [lambda: hand_over(1, "+", 0)],
            12: [lambda: hand_over(3, "-", 1)],
        },
        False,
    )

    for way, at in (("2", 2), ("+", 0), ("-", 1)):
        arrived(("n", way), rn.at[at])
    for half in (0, 1):
        for g in range(4):
            rows = slice(half * 512 + g * TOK, half * 512 + (g + 1) * TOK)
            at = slice(g * TOK, (g + 1) * TOK)
            denom = jnp.sum(oacc[0, rows, HD:] * eye, axis=0, keepdims=True)
            numer = oacc[0, rows, :HD]
            for n in range(3):
                denom += rn[n, half, 512 + g : 513 + g, :].astype(F32)
                numer += rn[n, half, at, :].astype(F32)
            inv = jnp.where(denom > 0, 1.0 / jnp.where(denom > 0, denom, 1.0), 0.0)
            inv = jnp.transpose(jnp.broadcast_to(inv, (TOK, TOK)))
            out_ref[:, (half * 4 + g) * HD : (half * 4 + g + 1) * HD] = (numer * inv).astype(BF16)

    for c in range(n_chunks):
        for k in range(8):
            copy_of(kv_c[c] + k, cs[c].at[k], cr[c].at[k], "c").wait_send()
    for key, (src, dst, peer) in started.items():
        copy_of(key, src(), dst(), peer).wait_send()


SEMAPHORES = 136


def per_device(
    image_rows, kv_weight, k_gain, tokens, ln_gain, q_weight, q_gain, image_doc, doc_first, doc_count, token_mask
):
    vmem = pl.BlockSpec(memory_space=pltpu.VMEM)
    hbm = pl.BlockSpec(memory_space=pl.ANY)
    width = kv_weight.shape[0]
    cols = q_weight.shape[1]
    rows = jnp.transpose(image_rows, (1, 0, 2))
    scratch = [
        pltpu.VMEM((1, HD), F32),
        pltpu.VMEM(tokens.shape, BF16),
        pltpu.VMEM((8, 8, 128), F32),
        pltpu.VMEM((1, HD), F32),
        pltpu.SMEM(image_doc.shape, jnp.int32),
        pltpu.SMEM(doc_first.shape, jnp.int32),
        pltpu.SMEM(doc_count.shape, jnp.int32),
        pltpu.VMEM((32, TOK), jnp.int32),
        pltpu.VMEM(rows.shape, BF16),
        pltpu.VMEM((IMG_ROWS, width), BF16),
        pltpu.VMEM((8, width, 2 * HD), BF16),
        pltpu.VMEM(q_weight.shape, BF16),
        pltpu.VMEM((8,) + tokens.shape, BF16),
        pltpu.VMEM((IMG_ROWS + 16, HD), F32),
        pltpu.VMEM((IMG_ROWS + 16, HD), F32),
        pltpu.VMEM((TOK, cols), F32),
        pltpu.VMEM((RING, 2, HALF, HD), BF16),
        pltpu.VMEM((RING, RING, TOK, HD), F32),
        pltpu.VMEM((RING, 2, KEYS, 3 * HD), BF16),
        pltpu.VMEM((RING, 8 * TOK, 2 * HD), F32),
        pltpu.VMEM((RING, 2, HALF, HD), BF16),
        pltpu.VMEM((3, 2, HALF, HD), BF16),
        pltpu.SemaphoreType.DMA((26,)),
        pltpu.SemaphoreType.DMA((SEMAPHORES,)),
        pltpu.SemaphoreType.DMA((SEMAPHORES,)),
        *[pltpu.VMEM((n, chunk.rows, 2 * HD), BF16) for n in (8, 8, 8, 6) for chunk in CHUNKS],
    ]
    return pl.pallas_call(
        kernel,
        out_shape=jax.ShapeDtypeStruct((tokens.shape[0], cols), BF16),
        in_specs=[hbm] * 11,
        out_specs=vmem,
        scratch_shapes=scratch,
        compiler_params=pltpu.CompilerParams(
            collective_id=0, has_side_effects=True, vmem_limit_bytes=62 * 2**20
        ),
        name="cross_attention",
    )(
        rows, kv_weight, k_gain.reshape(1, HD), tokens, ln_gain.reshape(8, 8, 128), q_weight,
        q_gain.reshape(1, HD), image_doc, doc_first, doc_count, token_mask.T,
    )


def solution(mesh):
    in_specs = (
        P("cp", None, ("segment", "tp")),
        P(("segment", "tp"), None),
        P(),
        P("cp", ("segment", "tp")),
        P(),
        P(None, ("segment", "tp")),
        P(),
        P(),
        P(),
        P(),
        P("cp", None),
    )
    out_specs = P("cp", ("segment", "tp"))
    return jax.shard_map(
        per_device, mesh=mesh, in_specs=in_specs, out_specs=out_specs, check_vma=False
    )
```

time: 520 us -> 75 us (0.14)
  the two profiles are of different devices: /device:TPU:3 before, /device:TPU:0 now
where the time goes in v3:
time: 75 us; the launch traced here: 74.8 us
  Pallas kernels  73.2 us (98%)
  local copies, waits for them, and re-layouts  1.67 us (2%)
    pallas_call x1, Pallas kernels, per_device(): pl.pallas_call(kernel, out_shape=jax.ShapeDtypeStruct((tokens.shape[0], c...  73.2 us
    unnamed x1, local copies, waits for them, and re-layouts  1.67 us

profile of v3, /device:TPU:0, one launch (start us, length us, event | category | flops | bytes accessed | tf_op | source)
XLA Modules:
  0.0 74.8 jit_solution(13769397234580588239)
XLA Ops:
  0.0 73.2 %cross_attention.1 = bf16[128,1024]{1,0:T(8,128)(2,1)} custom-call(bf16[801,2,1024]{2,1,0:T(2,128)(2,1)} %bitcast.5, bf16[1024,2048]{1,0:T(8,128)(2,1)} %w_hbm.1, f32[1,128]{1,0:T(1,128)} %bitcast.8, bf16[128,1024]{1,0:T(8,128)(2,1)} %tok_hbm.1, f32[8,8,128]{2,1,0:T(8,128)} %bitcast.6, bf16[8192,1024]{1,0:T(8,128)(2,1)} %wq_hbm.1, f32[1,128]{1,0:T(1,128)} %bitcast.9, ...), custom_call_target="tpu_custom_call" | custom-call | tf_op jit(solution)/shard_map/cross_attention/pallas_call | solution.py:507
  73.2 1.7 %copy.13 = bf16[128,1024]{1,0:T(8,128)(2,1)} copy(bf16[128,1024]{1,0:T(8,128)(2,1)} %cross_attention.1) | data formatting | bytes 524288

commit v4 on v3

--- a/solution.py
+++ b/solution.py
@@ -389,32 +389,32 @@
         chunk = CHUNKS[c]
         rows = pl.ds(chunk.key, chunk.keys)
 
-        def unit(u, carry):
+        def units(step, carry):
             for at, events in before.items():
-                @pl.when(u == at)
+                @pl.when(step * 2 == at)
                 def _():
                     for event in events:
                         event()
-            outer, inner = lax.div(u, RING), lax.rem(u, RING)
-            da, db = pick(outer if by_source else inner, SOURCES), pick(inner if by_source else outer, TARGETS)
-            src, dst = shard(da, 0), shard(0, db)
-            second = covered(2 * src + 1, dst)
-            weight = weights[da, db]
-            picked = jnp.where(second > 0, kvb[da, 1, rows, 0 : 2 * HD], kvb[da, 0, rows, 0 : 2 * HD])
-            keys = picked[:, :HD]
-            values = jnp.concatenate([picked[:, HD:], kvb[da, 0, rows, 2 * HD :]], axis=1)
-            for half in (0, 1):
-                scores = lax.dot_general(
-                    qall[db, half, :512, :], keys, (((1,), (1,)), ((), ())), preferred_element_type=F32
-                )
-                both = jnp.dot(jnp.exp2(scores).astype(BF16), values, preferred_element_type=F32)
-                for g in range(4):
-                    to = slice(half * 512 + g * TOK, half * 512 + (g + 1) * TOK)
-                    for cols in (slice(0, HD), slice(HD, 2 * HD)):
-                        oacc[db, to, cols] += both[g * TOK : (g + 1) * TOK, cols] * weight
+            for u in (step * 2, step * 2 + 1):
+                outer, inner = lax.div(u, RING), lax.rem(u, RING)
+                da, db = pick(outer if by_source else inner, SOURCES), pick(inner if by_source else outer, TARGETS)
+                second = covered(2 * shard(da, 0) + 1, shard(0, db))
+                weight = weights[da, db]
+                picked = jnp.where(second > 0, kvb[da, 1, rows, 0 : 2 * HD], kvb[da, 0, rows, 0 : 2 * HD])
+                keys = picked[:, :HD]
+                values = jnp.concatenate([picked[:, HD:], kvb[da, 0, rows, 2 * HD :]], axis=1)
+                for half in (0, 1):
+                    scores = lax.dot_general(
+                        qall[db, half, :512, :], keys, (((1,), (1,)), ((), ())), preferred_element_type=F32
+                    )
+                    both = jnp.dot(jnp.exp2(scores).astype(BF16), values, preferred_element_type=F32)
+                    for g in range(4):
+                        to = slice(half * 512 + g * TOK, half * 512 + (g + 1) * TOK)
+                        for cols in (slice(0, HD), slice(HD, 2 * HD)):
+                            oacc[db, to, cols] += both[g * TOK : (g + 1) * TOK, cols] * weight
             return carry
 
-        lax.fori_loop(0, RING * RING, unit, 0)
+        lax.fori_loop(0, RING * RING // 2, units, 0)
 
     for way, at in ways:
         arrived(("q", way), qall.at[at])
@@ -423,7 +423,7 @@
     attend(
         0,
         {
-            3: [lambda: kv_pass(1)],
+            2: [lambda: kv_pass(1)],
             4: [lambda: kv_forward(0, "+"), lambda: kv_forward(1, "-")],
             EARLY: [lambda: kv_finish(1)],
             12: [kv_forwarded],
@@ -433,9 +433,8 @@
     attend(
         1,
         {
-            1: [lambda: kv_gathered(1, "+")],
-            2: [lambda: kv_gathered(1, "-")],
-            3: [lambda: kv_gathered(1, "2")],
+            0: [lambda: kv_gathered(1, "+")],
+            2: [lambda: kv_gathered(1, "-"), lambda: kv_gathered(1, "2")],
             4: [lambda: hand_over(2, "2", 2)],
             8: [lambda: hand_over(1, "+", 0)],
             12: [lambda: hand_over(3, "-", 1)],

time: 75 us -> 74.1 us (0.988)
  Pallas kernels: 73.2 us -> 72.3 us
    pallas_call x1, Pallas kernels: 73.2 us -> 72.3 us  [per_device(): pl.pallas_call(kernel, out_shape=jax.ShapeDtypeStruct((tokens.shape[0], c...]
where the time goes in v4:
time: 74.1 us; the launch traced here: 74 us
  Pallas kernels  72.3 us (98%)
  local copies, waits for them, and re-layouts  1.67 us (2%)
    pallas_call x1, Pallas kernels, per_device(): pl.pallas_call(kernel, out_shape=jax.ShapeDtypeStruct((tokens.shape[0], c...  72.3 us
    unnamed x1, local copies, waits for them, and re-layouts  1.67 us

profile of v4, /device:TPU:0, one launch (start us, length us, event | category | flops | bytes accessed | tf_op | source)
XLA Modules:
  0.0 74.0 jit_solution(17787400854782152757)
XLA Ops:
  0.0 72.3 %cross_attention.1 = bf16[128,1024]{1,0:T(8,128)(2,1)} custom-call(bf16[801,2,1024]{2,1,0:T(2,128)(2,1)} %bitcast.5, bf16[1024,2048]{1,0:T(8,128)(2,1)} %w_hbm.1, f32[1,128]{1,0:T(1,128)} %bitcast.8, bf16[128,1024]{1,0:T(8,128)(2,1)} %tok_hbm.1, f32[8,8,128]{2,1,0:T(8,128)} %bitcast.6, bf16[8192,1024]{1,0:T(8,128)(2,1)} %wq_hbm.1, f32[1,128]{1,0:T(1,128)} %bitcast.9, ...), custom_call_target="tpu_custom_call" | custom-call | tf_op jit(solution)/shard_map/cross_attention/pallas_call | solution.py:506
  72.3 1.7 %copy.13 = bf16[128,1024]{1,0:T(8,128)(2,1)} copy(bf16[128,1024]{1,0:T(8,128)(2,1)} %cross_attention.1) | data formatting | bytes 524288
